TPU v7x, 256 devices: a whole 4x4x8 slice. The times are simulated.
256 devices in a mesh: slab: 4 (over x), dom: 64 (over z, y, core).
Axes of the slice: x: 4, y: 4, z: 8, core: 2. Of those that a mesh axis runs over, the one named last changes fastest.
Arguments:
- positions: float32 [3, 98304], P(None, ('slab', 'dom')), may hold values from -9 to 9
- species: int32 [98304], P(('slab', 'dom')), may hold values from 0 to 7
- domain: int32 [98304, 1], P(('slab', 'dom')), may hold values from 0 to 63; in each aligned block of 384 rows (0 to 383, 384 to 767, ...) at most 12 rows name the same one
- neighbours: int32 [16, 196608], P(None, ('slab', 'dom')), may hold values from 0 to 1535
- ghost_lists: int32 [2, 98304], P(None, ('slab', 'dom')), may hold values from 0 to 767, as said below
- embed_weight: bfloat16 [24, 256], replicated, may hold values from -1.25 to 1.25
- tensor_weight: bfloat16 [256, 32], replicated, may hold values from -0.375 to 0.375
- env_weight: bfloat16 [2, 256, 32], replicated, may hold values from -0.375 to 0.375
- scalar_mix: float32 [64, 32], replicated, may hold values from -0.75 to 0.75
- vector_mix: float32 [32, 32], replicated, may hold values from -1 to 1
- latent_weight: bfloat16 [2, 320, 256], replicated, may hold values from -0.3125 to 0.3125
- energy_weight: bfloat16 [256], replicated, may hold values from -0.375 to 0.375
Outputs:
- forces: float32 [3, 98304], P(None, ('slab', 'dom'))
- atom_energy: float32 [98304], P(('slab', 'dom'))
- atom_features: float32 [384, 98304], P(None, ('slab', 'dom'))
Inputs may be any that keep to these rules, and one draw needn't show every extreme that they name: Within the rows of one device at most 12 atoms name the same domain, and some domain takes exactly 12. `ghost_lists`: for each device, its blocks of the two rows together name each of its 768 slots exactly once.
All inputs are finite; a program needn't handle non-finite values.
Results may differ from a plain program's by a relative error of at most 0.02.
Values sent between devices are 32-bit elements; how exact they have to be, the bound alone decides.
A program may use at most 64 MiB of HBM per device.

v0:
```python
import jax
import jax.numpy as jnp
from jax import lax
from jax.sharding import PartitionSpec as P

BASIS = 8
SPECIES = 8


cutoff_radius = 5.0
soften = 0.25
neighbour_norm = 0.25
centre_block = 128
exact = lax.Precision.HIGHEST


def from_behind(value, axis, steps):
    count = lax.axis_size(axis)
    pairs = [(source, (source + steps) % count) for source in range(count)]
    return lax.ppermute(value, axis, pairs)


def envelope(scaled):
    return 1.0 - 28.0 * scaled**6 + 48.0 * scaled**7 - 21.0 * scaled**8


def block_terms(coords, kinds_float, first_slot, near_list, weights):
    (
        embed_weight,
        tensor_weight,
        env_weight,
        scalar_mix,
        vector_mix,
        latent_weight,
        energy_weight,
    ) = weights
    neigh_count, block_count = near_list.shape
    edge_count = neigh_count * block_count
    latent_width, chan_count = tensor_weight.shape
    column_count = coords.shape[1]
    centres = first_slot + jnp.arange(block_count)
    stacked = jnp.concatenate([coords, kinds_float[None]], axis=0)
    picker = (
        jnp.arange(column_count).astype(jnp.int32)[:, None] == near_list.reshape(1, edge_count)
    ).astype(jnp.float32)
    gathered = jnp.dot(stacked, picker, precision=exact).reshape(4, neigh_count, block_count)
    centre_cols = lax.dynamic_slice_in_dim(stacked, first_slot, block_count, 1)
    centre_xyz = centre_cols[:3]
    other_xyz = gathered[:3]
    centre_kind = centre_cols[3].astype(jnp.int32)
    other_kind = gathered[3].astype(jnp.int32)
    offset = other_xyz - centre_xyz[:, None, :]
    radius = jnp.sqrt(jnp.sum(offset * offset, axis=0) + soften)
    direction = offset / radius[None]
    scaled = jnp.minimum(radius / cutoff_radius, 1.0)
    smooth = envelope(scaled)
    live_edge = (centre_kind[None, :] >= 0) & (other_kind >= 0) & (near_list != centres[None, :])
    edge_weight = jnp.where(live_edge, smooth, jnp.zeros_like(smooth)).reshape(edge_count)
    orders = jnp.arange(1, BASIS + 1).astype(jnp.float32)
    radial_basis = (
        jnp.sin(jnp.pi * orders * scaled[..., None]) / scaled[..., None] * smooth[..., None]
    )
    kind_range = jnp.arange(SPECIES)
    centre_hot = (centre_kind[:, None] == kind_range).astype(jnp.float32)
    centre_hot = jnp.broadcast_to(centre_hot[None], (neigh_count, block_count, SPECIES))
    other_hot = (other_kind[..., None] == kind_range).astype(jnp.float32)
    inputs = jnp.concatenate([radial_basis, centre_hot, other_hot], axis=-1)
    inputs = inputs.astype(jnp.bfloat16).reshape(edge_count, BASIS + 2 * SPECIES)
    latent = jax.nn.silu(jnp.dot(inputs, embed_weight, preferred_element_type=jnp.float32)).astype(
        jnp.bfloat16
    )
    ones_row = jnp.ones((1, neigh_count, block_count), jnp.float32)
    harmonics = jnp.concatenate([ones_row, direction], axis=0).reshape(4, edge_count).T
    amplitude = jnp.dot(latent, tensor_weight, preferred_element_type=jnp.float32)
    tensor = harmonics[:, :, None] * amplitude[:, None, :]
    density = None
    for layer_index in range(2):
        env_amp = (
            jnp.dot(latent, env_weight[layer_index], preferred_element_type=jnp.float32)
            * edge_weight[:, None]
        )
        env_edge = harmonics[:, :, None] * env_amp[:, None, :]
        density = neighbour_norm * jnp.sum(
            env_edge.reshape(neigh_count, block_count, 4, chan_count), axis=0
        )
        spread = jnp.broadcast_to(density[None], (neigh_count, block_count, 4, chan_count))
        spread = spread.reshape(edge_count, 4, chan_count)
        scalars = jnp.concatenate(
            [tensor[:, 0] * spread[:, 0], jnp.sum(tensor[:, 1:] * spread[:, 1:], axis=1)], axis=-1
        )
        if layer_index == 0:
            vectors = tensor[:, :1] * spread[:, 1:] + tensor[:, 1:] * spread[:, :1]
            fresh_scalar = jnp.dot(scalars, scalar_mix, precision=exact)
            fresh_vector = jnp.einsum("emc,cd->emd", vectors, vector_mix, precision=exact)
            tensor = jnp.concatenate([fresh_scalar[:, None], fresh_vector], axis=1)
        joined = jnp.concatenate([latent, scalars.astype(jnp.bfloat16)], axis=-1)
        update = jax.nn.silu(
            jnp.dot(joined, latent_weight[layer_index], preferred_element_type=jnp.float32)
        )
        latent = (latent.astype(jnp.float32) + update).astype(jnp.bfloat16)
    edge_energy = jnp.dot(latent, energy_weight, preferred_element_type=jnp.float32) * edge_weight
    energy = jnp.sum(edge_energy.reshape(neigh_count, block_count), axis=0)
    weighted = (latent.astype(jnp.float32) * edge_weight[:, None]).reshape(
        neigh_count, block_count, latent_width
    )
    summary = neighbour_norm * jnp.sum(weighted, axis=0)
    features = jnp.concatenate([summary, density.reshape(block_count, 4 * chan_count)], axis=-1)
    return (energy, features)


def domain_forces(coords, kinds_float, near_lists, weights):
    slot_count = near_lists.shape[1]

    def block_step(carry, block_index):
        first_slot = block_index * centre_block
        near_list = lax.dynamic_slice_in_dim(near_lists, first_slot, centre_block, 1)

        def total_energy(positions_in):
            energy, features = block_terms(
                positions_in, kinds_float, first_slot, near_list, weights
            )
            return (jnp.sum(energy), (energy, features))

        gradient, (energy, features) = jax.grad(total_energy, has_aux=True)(coords)
        return (carry + gradient, (energy, features))

    block_ids = jnp.arange(slot_count // centre_block)
    gradient, (energy, features) = lax.scan(block_step, jnp.zeros_like(coords), block_ids)
    return (gradient, energy.reshape(slot_count), features.reshape(slot_count, features.shape[-1]))


def local(
    positions,
    species,
    domain,
    neighbours,
    ghost_lists,
    embed_weight,
    tensor_weight,
    env_weight,
    scalar_mix,
    vector_mix,
    latent_weight,
    energy_weight,
):
    weights = (
        embed_weight,
        tensor_weight,
        env_weight,
        scalar_mix,
        vector_mix,
        latent_weight,
        energy_weight,
    )
    domains = lax.axis_size("dom")
    atom_count = positions.shape[1]
    slot_count = 2 * atom_count
    capacity = slot_count // domains
    target = domain[:, 0]
    one_hot = (target[:, None] == jnp.arange(domains)).astype(jnp.float32)
    atom_range = jnp.arange(atom_count)
    earlier = (atom_range[:, None] > atom_range[None, :]).astype(jnp.float32)
    before = jnp.dot(earlier, one_hot, precision=exact)
    order_rank = jnp.sum(one_hot * before, axis=1).astype(jnp.int32)
    placement = target * capacity + order_rank
    slot_range = jnp.arange(slot_count)
    place_hot = (slot_range[:, None] == placement[None, :]).astype(jnp.float32)
    occupied = jnp.sum(place_hot, axis=1)
    packed = jnp.concatenate([positions, species[None].astype(jnp.float32)], axis=0)
    moved = jnp.dot(packed, place_hot.T, precision=exact)
    moved = jnp.concatenate([moved[:3], moved[3:] + occupied[None] - 1.0], axis=0)
    outgoing = moved.reshape(4, domains, capacity)
    arrived = lax.all_to_all(outgoing, "dom", split_axis=1, concat_axis=1, tiled=True)
    own_cols = arrived.reshape(4, slot_count)
    lower_list = ghost_lists[0]
    upper_list = ghost_lists[1]
    ghost_count = lower_list.shape[0]
    down_hot = (slot_range[:, None] == lower_list[None, :]).astype(jnp.float32)
    up_hot = (slot_range[:, None] == upper_list[None, :]).astype(jnp.float32)
    lend_down = jnp.dot(own_cols, down_hot, precision=exact)
    lend_up = jnp.dot(own_cols, up_hot, precision=exact)
    from_lower = from_behind(lend_up, ("slab", "dom"), 1)
    from_upper = from_behind(lend_down, ("slab", "dom"), -1)
    extended_cols = jnp.concatenate([own_cols, from_lower, from_upper], axis=1)
    ext_pos = extended_cols[:3]
    ext_kind = extended_cols[3]
    gradient, energy, features = domain_forces(ext_pos, ext_kind, neighbours, weights)
    own_grad = gradient[:, :slot_count]
    lower_back = gradient[:, slot_count : slot_count + ghost_count]
    upper_back = gradient[:, slot_count + ghost_count :]
    onto_upper = from_behind(lower_back, ("slab", "dom"), -1)
    onto_lower = from_behind(upper_back, ("slab", "dom"), 1)
    total_grad = own_grad + jnp.dot(onto_upper, up_hot.T, precision=exact)
    total_grad = total_grad + jnp.dot(onto_lower, down_hot.T, precision=exact)
    results = jnp.concatenate([-total_grad, energy[None]], axis=0).reshape(4, domains, capacity)
    feature_cols = features.T.reshape(features.shape[1], domains, capacity)
    home_features, home_results = (
        lax.all_to_all(feature_cols, "dom", split_axis=1, concat_axis=1, tiled=True),
        lax.all_to_all(results, "dom", split_axis=1, concat_axis=1, tiled=True),
    )
    picked = jnp.dot(home_results.reshape(4, slot_count), place_hot, precision=exact)
    atom_features = jnp.dot(
        home_features.reshape(features.shape[1], slot_count), place_hot, precision=exact
    )
    return (picked[:3], picked[3], atom_features)


def solution(mesh):
    in_specs = (
        P(None, ("slab", "dom")),
        P(("slab", "dom")),
        P(("slab", "dom"), None),
        P(None, ("slab", "dom")),
        P(None, ("slab", "dom")),
        P(),
        P(),
        P(),
        P(),
        P(),
        P(),
        P(),
    )
    out_specs = (P(None, ("slab", "dom")), P(("slab", "dom")), P(None, ("slab", "dom")))
    return jax.shard_map(local, mesh=mesh, in_specs=in_specs, out_specs=out_specs, check_vma=False)
```

profile of v0, /device:TPU:1, one launch (start us, length us, event | category | flops | bytes accessed | tf_op | source)
XLA Modules:
  0.0 472.2 jit_solution(16909207841628495631)
XLA Ops:
  4.8 13.2 %all-to-all-start = ((f32[4,64,12]{2,0,1:T(4,128)}), f32[4,64,12]{2,0,1:T(4,128)S(1)}, u32[]{:S(2)}, u32[]{:S(2)}) async-start(f32[4,64,12]{2,0,1:T(4,128)} %copy.126), calls=%async_computation | async-start | bytes 262144 | tf_op jit(solution)/shard_map/all_to_all | solution.py:173
  18.7 10.3 %all-to-all-done = f32[4,64,12]{2,0,1:T(4,128)S(1)} async-done(((f32[4,64,12]{2,0,1:T(4,128)}), f32[4,64,12]{2,0,1:T(4,128)S(1)}, u32[]{:S(2)}, u32[]{:S(2)}) %all-to-all-start) | async-done | bytes 12320 | tf_op jit(solution)/shard_map/all_to_all | solution.py:173
  35.1 355.2 %while.17 = (s32[]{:T(128)}, f32[3,1536]{1,0:T(4,128)}, f32[6,128]{1,0:T(8,128)}, f32[6,128,384]{2,1,0:T(8,128)}, s32[6]{0:T(128)S(1)}, /*index=5*/s32[16,768]{1...) while((s32[]{:T(128)}, f32[3,1536]{1,0:T(4,128)}, ...), condition=%wide.region_27.28_spmd.clone, body=%wide.region_2.27_spmd.clone.sunk | while | flops 2210399232 | bytes 169835936 | solution.py:128
  38.0 4.7 fusion.259
  45.1 2.0 multiply_convert_fusion.9
  53.3 2.3 add_convert_fusion.4
  62.5 2.0 multiply_bitcast_fusion.27
  70.8 1.9 multiply_reduce_fusion.28
  81.6 3.6 fusion.271
  85.9 5.6 %fusion.276 = f32[4,1536]{1,0:T(4,128)S(1)} fusion(s32[2048]{0:T(1024)S(1)} %copy-done.48, f32[1,4,16,128]{3,2,1,0:T(8,128)S(1)} %pad_bitcast_fusion.5), kind=kOutput, calls=%fused_computation.1.clone.1 | convolution fusion | flops 154140672 | bytes 65536 | tf_op jit(solution)/shard_map/while/body/eval_jaxpr/transpose(jvp())/dot_general | solution.py:46
  97.1 4.7 fusion.259
  104.3 2.0 multiply_convert_fusion.9
  112.5 2.3 add_convert_fusion.4
  121.6 2.0 multiply_bitcast_fusion.27
  129.9 1.9 multiply_reduce_fusion.28
  140.7 3.6 fusion.271
  145.0 5.6 %fusion.276 = f32[4,1536]{1,0:T(4,128)S(1)} fusion(s32[2048]{0:T(1024)S(1)} %copy-done.48, f32[1,4,16,128]{3,2,1,0:T(8,128)S(1)} %pad_bitcast_fusion.5), kind=kOutput, calls=%fused_computation.1.clone.1 | convolution fusion | flops 154140672 | bytes 65536 | tf_op jit(solution)/shard_map/while/body/eval_jaxpr/transpose(jvp())/dot_general | solution.py:46
  156.3 4.7 fusion.259
  163.4 2.0 multiply_convert_fusion.9
  171.6 2.3 add_convert_fusion.4
  180.8 2.0 multiply_bitcast_fusion.27
  189.1 1.9 multiply_reduce_fusion.28
  199.9 3.6 fusion.271
  204.2 5.6 %fusion.276 = f32[4,1536]{1,0:T(4,128)S(1)} fusion(s32[2048]{0:T(1024)S(1)} %copy-done.48, f32[1,4,16,128]{3,2,1,0:T(8,128)S(1)} %pad_bitcast_fusion.5), kind=kOutput, calls=%fused_computation.1.clone.1 | convolution fusion | flops 154140672 | bytes 65536 | tf_op jit(solution)/shard_map/while/body/eval_jaxpr/transpose(jvp())/dot_general | solution.py:46
  215.5 4.7 fusion.259
  222.6 2.0 multiply_convert_fusion.9
  230.8 2.3 add_convert_fusion.4
  240.0 2.0 multiply_bitcast_fusion.27
  259.1 3.6 fusion.271
  263.4 5.6 %fusion.276 = f32[4,1536]{1,0:T(4,128)S(1)} fusion(s32[2048]{0:T(1024)S(1)} %copy-done.48, f32[1,4,16,128]{3,2,1,0:T(8,128)S(1)} %pad_bitcast_fusion.5), kind=kOutput, calls=%fused_computation.1.clone.1 | convolution fusion | flops 154140672 | bytes 65536 | tf_op jit(solution)/shard_map/while/body/eval_jaxpr/transpose(jvp())/dot_general | solution.py:46
  274.7 4.7 fusion.259
  281.8 2.0 multiply_convert_fusion.9
  290.0 2.3 add_convert_fusion.4
  299.2 2.0 multiply_bitcast_fusion.27
  318.3 3.6 fusion.271
  322.6 5.6 %fusion.276 = f32[4,1536]{1,0:T(4,128)S(1)} fusion(s32[2048]{0:T(1024)S(1)} %copy-done.48, f32[1,4,16,128]{3,2,1,0:T(8,128)S(1)} %pad_bitcast_fusion.5), kind=kOutput, calls=%fused_computation.1.clone.1 | convolution fusion | flops 154140672 | bytes 65536 | tf_op jit(solution)/shard_map/while/body/eval_jaxpr/transpose(jvp())/dot_general | solution.py:46
  333.8 4.7 fusion.259
  340.9 2.0 multiply_convert_fusion.9
  349.1 2.3 add_convert_fusion.4
  358.3 2.0 multiply_bitcast_fusion.27
  377.4 3.6 fusion.271
  381.7 5.6 %fusion.276 = f32[4,1536]{1,0:T(4,128)S(1)} fusion(s32[2048]{0:T(1024)S(1)} %copy-done.48, f32[1,4,16,128]{3,2,1,0:T(8,128)S(1)} %pad_bitcast_fusion.5), kind=kOutput, calls=%fused_computation.1.clone.1 | convolution fusion | flops 154140672 | bytes 65536 | tf_op jit(solution)/shard_map/while/body/eval_jaxpr/transpose(jvp())/dot_general | solution.py:46
  392.5 7.4 %collective-permute-start.2 = (f32[3,384]{1,0:T(4,128)S(1)}, f32[3,384]{1,0:T(4,128)S(1)}, u32[]{:S(2)}, u32[]{:S(2)}) collective-permute-start(f32[3,384]{1,0:T(4,128)S(1)} %get-tuple-element.305), channel_id=1, source_target_pairs={{0,255},{1,0},{2,1},{3,2},{4,3},{5,4},{6,5},{7,6},{8,7},{9,8},{10,... | collective-permute-start | bytes 13832 | tf_op jit(solution)/shard_map/ppermute | solution.py:20
  403.4 11.7 %all-to-all-start.1 = ((f32[4,64,12]{2,0,1:T(4,128)}), f32[4,64,12]{2,0,1:T(4,128)S(1)}, u32[]{:S(2)}, u32[]{:S(2)}) async-start(f32[4,64,12]{2,0,1:T(4,128)} %copy.128), calls=%async_computation.1 | async-start | bytes 262144 | tf_op jit(solution)/shard_map/all_to_all | solution.py:199
  416.4 10.1 %all-to-all-done.1 = f32[4,64,12]{2,0,1:T(4,128)S(1)} async-done(((f32[4,64,12]{2,0,1:T(4,128)}), f32[4,64,12]{2,0,1:T(4,128)S(1)}, u32[]{:S(2)}, u32[]{:S(2)}) %all-to-all-start.1) | async-done | bytes 12320 | tf_op jit(solution)/shard_map/all_to_all | solution.py:199
  426.4 4.5 all-to-all-start.2
  432.2 37.9 %all-to-all-done.2 = f32[384,64,12]{0,2,1:T(8,128)S(1)} async-done(((f32[384,64,12]{0,2,1:T(8,128)}), f32[384,64,12]{0,2,1:T(8,128)S(1)}, u32[]{:S(2)}, u32[]{:S(2)}) %all-to-all-start.2) | async-done | bytes 1179680 | tf_op jit(solution)/shard_map/all_to_all | solution.py:198
  470.2 2.0 fusion.136
  (1278 shorter events, 237.5 us)
Async XLA Ops:
  0.6 34.5 %copy-start.60 = (bf16[24,256]{1,0:T(8,128)(2,1)S(1)}, bf16[24,256]{1,0:T(8,128)(2,1)}, u32[]{:S(2)}) copy-start(bf16[24,256]{1,0:T(8,128)(2,1)} %param.19) | copy-start | bytes 36868
  0.6 34.5 %copy-start.31 = (bf16[256,32]{0,1:T(8,128)(2,1)S(1)}, bf16[256,32]{0,1:T(8,128)(2,1)}, u32[]{:S(2)}) copy-start(bf16[256,32]{0,1:T(8,128)(2,1)} %param.20) | copy-start | bytes 49156
  1.6 17.1 %copy-start.52 = (s32[384]{0:T(512)}, s32[384]{0:T(512)S(1)}, u32[]{:S(2)}) copy-start(s32[384]{0:T(512)S(1)} %convert_add_fusion) | copy-start | bytes 4612
  4.8 24.3 %all-to-all-start = ((f32[4,64,12]{2,0,1:T(4,128)}), f32[4,64,12]{2,0,1:T(4,128)S(1)}, u32[]{:S(2)}, u32[]{:S(2)}) async-start(f32[4,64,12]{2,0,1:T(4,128)} %copy.126), calls=%async_computation | async-start | bytes 262144 | tf_op jit(solution)/shard_map/all_to_all | solution.py:173
  18.7 16.4 %copy-start.54 = (s32[384]{0:T(512)}, s32[384]{0:T(512)S(1)}, u32[]{:S(2)}) copy-start(s32[384]{0:T(512)S(1)} %get-tuple-element.232) | copy-start | bytes 4612
  18.7 16.4 %copy-start.55 = (s32[384]{0:T(512)}, s32[384]{0:T(512)S(1)}, u32[]{:S(2)}) copy-start(s32[384]{0:T(512)S(1)} %get-tuple-element.233) | copy-start | bytes 4612
  29.6 3.1 collective-permute-start.1
  30.5 4.0 collective-permute-start
  37.3 5.3 %copy-start.47 = (s32[2048]{0:T(1024)}, s32[2048]{0:T(1024)S(1)}, u32[]{:S(2)}) copy-start(s32[2048]{0:T(1024)S(1)} %dynamic-slice_bitcast_fusion.2) | copy-start | bytes 24580 | tf_op jit(solution)/shard_map/while
  38.0 9.4 %copy-start.37 = (f32[4,128]{1,0:T(4,128)}, f32[4,128]{1,0:T(4,128)S(1)}, u32[]{:S(2)}) copy-start(f32[4,128]{1,0:T(4,128)S(1)} %constant_dynamic-slice_fusion.2) | copy-start | bytes 6148 | tf_op jit(solution)/shard_map/while
  69.8 4.7 copy-start.67
  85.7 5.8 %copy-start.45 = (f32[3,1536]{1,0:T(4,128)S(1)}, f32[3,1536]{1,0:T(4,128)}, u32[]{:S(2)}) copy-start(f32[3,1536]{1,0:T(4,128)} %get-tuple-element.519) | copy-start | bytes 55300 | tf_op jit(solution)/shard_map/while
  85.7 7.1 %copy-start = (f32[32,8,16,128]{3,1,2,0:T(8,128)S(1)}, f32[32,8,16,128]{3,1,2,0:T(8,128)}, u32[]{:S(2)}) copy-start(f32[32,8,16,128]{3,1,2,0:T(8,128)} %get-tuple-element.497) | copy-start | bytes 6291460 | tf_op jit(solution)/shard_map/while
  96.4 5.4 %copy-start.47 = (s32[2048]{0:T(1024)}, s32[2048]{0:T(1024)S(1)}, u32[]{:S(2)}) copy-start(s32[2048]{0:T(1024)S(1)} %dynamic-slice_bitcast_fusion.2) | copy-start | bytes 24580 | tf_op jit(solution)/shard_map/while
  97.1 9.4 %copy-start.37 = (f32[4,128]{1,0:T(4,128)}, f32[4,128]{1,0:T(4,128)S(1)}, u32[]{:S(2)}) copy-start(f32[4,128]{1,0:T(4,128)S(1)} %constant_dynamic-slice_fusion.2) | copy-start | bytes 6148 | tf_op jit(solution)/shard_map/while
  128.9 4.7 copy-start.59
  128.9 4.7 copy-start.67
  144.8 5.8 %copy-start.45 = (f32[3,1536]{1,0:T(4,128)S(1)}, f32[3,1536]{1,0:T(4,128)}, u32[]{:S(2)}) copy-start(f32[3,1536]{1,0:T(4,128)} %get-tuple-element.519) | copy-start | bytes 55300 | tf_op jit(solution)/shard_map/while
  144.8 7.1 %copy-start = (f32[32,8,16,128]{3,1,2,0:T(8,128)S(1)}, f32[32,8,16,128]{3,1,2,0:T(8,128)}, u32[]{:S(2)}) copy-start(f32[32,8,16,128]{3,1,2,0:T(8,128)} %get-tuple-element.497) | copy-start | bytes 6291460 | tf_op jit(solution)/shard_map/while
  155.6 5.3 %copy-start.47 = (s32[2048]{0:T(1024)}, s32[2048]{0:T(1024)S(1)}, u32[]{:S(2)}) copy-start(s32[2048]{0:T(1024)S(1)} %dynamic-slice_bitcast_fusion.2) | copy-start | bytes 24580 | tf_op jit(solution)/shard_map/while
  156.3 9.4 %copy-start.37 = (f32[4,128]{1,0:T(4,128)}, f32[4,128]{1,0:T(4,128)S(1)}, u32[]{:S(2)}) copy-start(f32[4,128]{1,0:T(4,128)S(1)} %constant_dynamic-slice_fusion.2) | copy-start | bytes 6148 | tf_op jit(solution)/shard_map/while
  188.1 4.7 copy-start.67
  204.0 5.8 %copy-start.45 = (f32[3,1536]{1,0:T(4,128)S(1)}, f32[3,1536]{1,0:T(4,128)}, u32[]{:S(2)}) copy-start(f32[3,1536]{1,0:T(4,128)} %get-tuple-element.519) | copy-start | bytes 55300 | tf_op jit(solution)/shard_map/while
  204.0 7.1 %copy-start = (f32[32,8,16,128]{3,1,2,0:T(8,128)S(1)}, f32[32,8,16,128]{3,1,2,0:T(8,128)}, u32[]{:S(2)}) copy-start(f32[32,8,16,128]{3,1,2,0:T(8,128)} %get-tuple-element.497) | copy-start | bytes 6291460 | tf_op jit(solution)/shard_map/while
  214.8 5.4 %copy-start.47 = (s32[2048]{0:T(1024)}, s32[2048]{0:T(1024)S(1)}, u32[]{:S(2)}) copy-start(s32[2048]{0:T(1024)S(1)} %dynamic-slice_bitcast_fusion.2) | copy-start | bytes 24580 | tf_op jit(solution)/shard_map/while
  215.5 9.4 %copy-start.37 = (f32[4,128]{1,0:T(4,128)}, f32[4,128]{1,0:T(4,128)S(1)}, u32[]{:S(2)}) copy-start(f32[4,128]{1,0:T(4,128)S(1)} %constant_dynamic-slice_fusion.2) | copy-start | bytes 6148 | tf_op jit(solution)/shard_map/while
  247.2 4.7 copy-start.59
  247.2 4.7 copy-start.67
  263.2 5.8 %copy-start.45 = (f32[3,1536]{1,0:T(4,128)S(1)}, f32[3,1536]{1,0:T(4,128)}, u32[]{:S(2)}) copy-start(f32[3,1536]{1,0:T(4,128)} %get-tuple-element.519) | copy-start | bytes 55300 | tf_op jit(solution)/shard_map/while
  263.2 7.1 %copy-start = (f32[32,8,16,128]{3,1,2,0:T(8,128)S(1)}, f32[32,8,16,128]{3,1,2,0:T(8,128)}, u32[]{:S(2)}) copy-start(f32[32,8,16,128]{3,1,2,0:T(8,128)} %get-tuple-element.497) | copy-start | bytes 6291460 | tf_op jit(solution)/shard_map/while
  274.0 5.4 %copy-start.47 = (s32[2048]{0:T(1024)}, s32[2048]{0:T(1024)S(1)}, u32[]{:S(2)}) copy-start(s32[2048]{0:T(1024)S(1)} %dynamic-slice_bitcast_fusion.2) | copy-start | bytes 24580 | tf_op jit(solution)/shard_map/while
  274.7 9.4 %copy-start.37 = (f32[4,128]{1,0:T(4,128)}, f32[4,128]{1,0:T(4,128)S(1)}, u32[]{:S(2)}) copy-start(f32[4,128]{1,0:T(4,128)S(1)} %constant_dynamic-slice_fusion.2) | copy-start | bytes 6148 | tf_op jit(solution)/shard_map/while
  306.5 4.7 copy-start.67
  322.4 5.8 %copy-start.45 = (f32[3,1536]{1,0:T(4,128)S(1)}, f32[3,1536]{1,0:T(4,128)}, u32[]{:S(2)}) copy-start(f32[3,1536]{1,0:T(4,128)} %get-tuple-element.519) | copy-start | bytes 55300 | tf_op jit(solution)/shard_map/while
  322.4 7.1 %copy-start = (f32[32,8,16,128]{3,1,2,0:T(8,128)S(1)}, f32[32,8,16,128]{3,1,2,0:T(8,128)}, u32[]{:S(2)}) copy-start(f32[32,8,16,128]{3,1,2,0:T(8,128)} %get-tuple-element.497) | copy-start | bytes 6291460 | tf_op jit(solution)/shard_map/while
  333.2 5.3 %copy-start.47 = (s32[2048]{0:T(1024)}, s32[2048]{0:T(1024)S(1)}, u32[]{:S(2)}) copy-start(s32[2048]{0:T(1024)S(1)} %dynamic-slice_bitcast_fusion.2) | copy-start | bytes 24580 | tf_op jit(solution)/shard_map/while
  333.8 9.4 %copy-start.37 = (f32[4,128]{1,0:T(4,128)}, f32[4,128]{1,0:T(4,128)S(1)}, u32[]{:S(2)}) copy-start(f32[4,128]{1,0:T(4,128)S(1)} %constant_dynamic-slice_fusion.2) | copy-start | bytes 6148 | tf_op jit(solution)/shard_map/while
  365.6 4.7 copy-start.59
  365.6 4.7 copy-start.67
  381.5 5.8 %copy-start.45 = (f32[3,1536]{1,0:T(4,128)S(1)}, f32[3,1536]{1,0:T(4,128)}, u32[]{:S(2)}) copy-start(f32[3,1536]{1,0:T(4,128)} %get-tuple-element.519) | copy-start | bytes 55300 | tf_op jit(solution)/shard_map/while
  381.5 7.1 %copy-start = (f32[32,8,16,128]{3,1,2,0:T(8,128)S(1)}, f32[32,8,16,128]{3,1,2,0:T(8,128)}, u32[]{:S(2)}) copy-start(f32[32,8,16,128]{3,1,2,0:T(8,128)} %get-tuple-element.497) | copy-start | bytes 6291460 | tf_op jit(solution)/shard_map/while
  390.4 24.7 %copy-start.35 = (f32[6,128,384]{2,1,0:T(8,128)S(1)}, f32[6,128,384]{2,1,0:T(8,128)}, u32[]{:S(2)}) copy-start(f32[6,128,384]{2,1,0:T(8,128)} %get-tuple-element.589) | copy-start | bytes 3538948
  391.2 8.7 %collective-permute-start.3 = (f32[3,384]{1,0:T(4,128)S(1)}, f32[3,384]{1,0:T(4,128)S(1)}, u32[]{:S(2)}, u32[]{:S(2)}) collective-permute-start(f32[3,384]{1,0:T(4,128)S(1)} %get-tuple-element.306), channel_id=1, source_target_pairs={{0,1},{1,2},{2,3},{3,4},{4,5},{5,6},{6,7},{7,8},{8,9},{9,10},{10,1... | collective-permute-start | bytes 13832 | tf_op jit(solution)/shard_map/ppermute | solution.py:20
  392.5 8.7 %collective-permute-start.2 = (f32[3,384]{1,0:T(4,128)S(1)}, f32[3,384]{1,0:T(4,128)S(1)}, u32[]{:S(2)}, u32[]{:S(2)}) collective-permute-start(f32[3,384]{1,0:T(4,128)S(1)} %get-tuple-element.305), channel_id=1, source_target_pairs={{0,255},{1,0},{2,1},{3,2},{4,3},{5,4},{6,5},{7,6},{8,7},{9,8},{10,... | collective-permute-start | bytes 13832 | tf_op jit(solution)/shard_map/ppermute | solution.py:20
  403.4 23.0 %all-to-all-start.1 = ((f32[4,64,12]{2,0,1:T(4,128)}), f32[4,64,12]{2,0,1:T(4,128)S(1)}, u32[]{:S(2)}, u32[]{:S(2)}) async-start(f32[4,64,12]{2,0,1:T(4,128)} %copy.128), calls=%async_computation.1 | async-start | bytes 262144 | tf_op jit(solution)/shard_map/all_to_all | solution.py:199
  416.4 14.7 %copy-start.53 = (s32[384]{0:T(512)S(1)}, s32[384]{0:T(512)}, u32[]{:S(2)}) copy-start(s32[384]{0:T(512)} %copy-done.52) | copy-start | bytes 4612
  426.4 43.6 %all-to-all-start.2 = ((f32[384,64,12]{0,2,1:T(8,128)}), f32[384,64,12]{0,2,1:T(8,128)S(1)}, u32[]{:S(2)}, u32[]{:S(2)}) async-start(f32[384,64,12]{0,2,1:T(8,128)} %reshape.432), calls=%async_computation.2 | async-start | bytes 3145728 | tf_op jit(solution)/shard_map/all_to_all | solution.py:198
  431.6 40.6 %copy-start.56 = (f32[4,384]{1,0:T(4,128)}, f32[4,384]{1,0:T(4,128)S(1)}, u32[]{:S(2)}) copy-start(f32[4,384]{1,0:T(4,128)S(1)} %fusion.137) | copy-start | bytes 18436
  (327 other events, 715.7 us)
where the time goes:
time: 479 us; the launch traced here: 472 us
  matrix products  191 us (40%)
  local copies, waits for them, and re-layouts  97.3 us (20%)
  other arithmetic  72.8 us (15%)
  waiting for transfers between devices  60.8 us (13%)
  starting transfers between devices  39.1 us (8%)
  loops' own time  10.2 us (2%)
    dot_general x12, matrix products, block_terms(): jnp.dot(stacked, picker, precision=exact)  61.5 us
    all_to_all x1, waiting for transfers between devices, local(): lax.all_to_all(feature_cols, 'dom', split_axis=1, concat_axis=1, tiled=True)  37.9 us
    while x774, local copies, waits for them, and re-layouts  37.1 us
    dot_general x12, matrix products, block_terms(): jnp.dot(inputs, embed_weight, preferred_element_type=jnp.float32)  33.6 us
    dot_general x24, matrix products, block_terms(): jnp.dot(joined, latent_weight[layer_index], preferred_element_type=jnp.fl...  32.4 us
    dot_general x18, matrix products, block_terms(): jnp.dot(latent, env_weight[layer_index], preferred_element_type=jnp.float32)  18.4 us
    dot_general x12, matrix products, block_terms(): jnp.einsum('emc,cd->emd', vectors, vector_mix, precision=exact)  17.6 us
    reshape x12, local copies, waits for them, and re-layouts, block_terms(): spread = spread.reshape(edge_count, 4, chan_count)  16.6 us
  transfers between devices with their start and end apart: 7, of which 5 were waited for; matrix products, arithmetic and copies ran while one was open for 1% of the time, Pallas kernels for 0%

commit v1 on v0

v1 whole, which is shorter than its diff:
```python
import math

import jax
import jax.numpy as jnp
from jax import lax
from jax.experimental import pallas as pl
from jax.experimental.pallas import tpu as pltpu
from jax.sharding import PartitionSpec as P

F32 = jnp.float32
BF16 = jnp.bfloat16
LANES = 128
WIDE = 256
NEIGH = 16
UNROLL = 4


def mm(a, b):
    return jnp.dot(a, b, preferred_element_type=F32)


def silu_parts(half):
    gate = jnp.tanh(half)
    rise = 1.0 + gate
    value = half * rise
    slope = rise + value * (1.0 - gate)
    return value, slope


def arrange_weights(
    embed_weight, tensor_weight, env_weight, scalar_mix, vector_mix, latent_weight, energy_weight,
    w_in, w_first, w_mix, w_second, w_third, w_energy, b_second, b_mix, b_first, b_amp, b_in, stage,
):
    width, chan = tensor_weight.shape
    lat0, lat1 = latent_weight[0].astype(F32) * 0.5, latent_weight[1].astype(F32) * 0.5
    b_first[...] = lat0.astype(BF16)
    b_second[...] = lat1.astype(BF16)
    small = jnp.concatenate(
        [tensor_weight[...], env_weight[0], env_weight[1], jnp.zeros((width, chan), BF16)], axis=1)
    b_amp[...] = small[:, :64]
    small = small.astype(F32).T.astype(BF16)
    w_first[0:64] = small[0:64]
    w_first[64:] = lat0[:width].T.astype(BF16)
    w_second[0:32] = small[64:96]
    w_second[32:] = lat1[:width].T.astype(BF16)
    w_third[...] = lat1[width:].T.astype(BF16)
    embed = embed_weight[...].astype(F32) * 0.5
    b_in[...] = embed[:16].astype(BF16)
    w_in[...] = jnp.concatenate([embed, jnp.zeros((8, width), F32)], axis=0).T.astype(BF16)
    w_energy[...] = jnp.broadcast_to(energy_weight[...].astype(F32), (8, width)).T[:, 0:1] + jnp.zeros((width, WIDE), F32)
    stage[...] = jnp.zeros_like(stage)
    stage[0:64, 0:32] = scalar_mix[...]
    for m in range(3):
        stage[64 + 32 * m:96 + 32 * m, 32 + 32 * m:64 + 32 * m] = vector_mix[...]
    core = stage[...]
    b_mix[...] = jnp.zeros_like(b_mix)
    b_mix[0:width, 0:32] = env_weight[1]
    b_mix[width:, 32:] = core[0:160].astype(BF16)
    w_mix[...] = jnp.zeros_like(w_mix)
    w_mix[0:width, 0:64] = w_third_like(lat0[width:])
    w_mix[width:] = core.T[:, 0:160].astype(BF16)


def w_third_like(part):
    return part.T.astype(BF16)


def force_kernel(
    ext, near, embed_weight, tensor_weight, env_weight, scalar_mix, vector_mix, latent_weight, energy_weight,
    grad_out, energy_out, feature_out,
    w_in, w_first, w_mix, w_second, w_third, w_energy, b_second, b_mix, b_first, b_amp, b_in, stage,
    geo, kind_hot, lat0, slope0, half0, amp, tens, envl, lat1, slope1, half1, dlat, dscal, damp, back,
    dens0, dens1, ddens0, ddens1, summary, ghost_acc, centre_acc, energy_acc,
):
    blocks = geo.shape[0]
    own = ext
    slots = blocks * WIDE
    sub = ext.shape[1] // LANES
    arrange_weights(
        embed_weight, tensor_weight, env_weight, scalar_mix, vector_mix, latent_weight, energy_weight,
        w_in, w_first, w_mix, w_second, w_third, w_energy, b_second, b_mix, b_first, b_amp, b_in, stage)
    ghost_acc[...] = jnp.zeros_like(ghost_acc)

    for piece in range(blocks * WIDE // LANES):
        b, half = piece // 2, piece % 2
        lanes = pl.ds(half * LANES, LANES)
        index = near[:, piece * LANES:(piece + 1) * LANES]
        low = jnp.bitwise_and(index, LANES - 1)
        high = jnp.right_shift(index, 7)
        got = []
        for comp in range(4):
            value = jnp.zeros((NEIGH, LANES), F32)
            for h in range(sub):
                row = jnp.broadcast_to(ext[comp:comp + 1, h * LANES:(h + 1) * LANES], (NEIGH, LANES))
                taken = jnp.take_along_axis(row, low, axis=1)
                value = jnp.where(high == h, taken, value)
            got.append(value)
        mine = [own[c:c + 1, piece * LANES:(piece + 1) * LANES] for c in range(4)]
        off = [got[c] - mine[c] for c in range(3)]
        radius = jnp.sqrt(off[0] * off[0] + off[1] * off[1] + off[2] * off[2] + 0.25)
        inv = 1.0 / radius
        x = jnp.minimum(radius * 0.2, 1.0)
        x2 = x * x
        x3 = x2 * x
        x5 = x2 * x3
        u = 1.0 + x3 * x3 * (-28.0 + x * (48.0 - 21.0 * x))
        du = -168.0 * x5 * (1.0 - x) * (1.0 - x)
        du = jnp.where(radius < 5.0, du, 0.0)
        slot = piece * LANES + lax.broadcasted_iota(jnp.int32, (NEIGH, LANES), 1)
        live = (mine[3] >= 0.0) & (got[3] >= 0.0) & (index != slot)
        w = jnp.where(live, u, 0.0)
        items = [w, off[0] * inv, off[1] * inv, off[2] * inv, x, u, du, inv, got[3],
                 jnp.where(radius < 5.0, 0.2, 0.0), jnp.where(live, du, 0.0)]
        for c, item in enumerate(items):
            geo[b, c, :, lanes] = item

    def row(b, c, k):
        return geo[b, c, pl.ds(k, 1), :]

    @pl.loop(0, blocks)
    def _(b):
        start = pl.multiple_of(b * WIDE, WIDE)
        eight = lax.broadcasted_iota(jnp.int32, (8, WIDE), 0).astype(F32)
        my_kind = own[3:4, pl.ds(start, WIDE)]
        kind_hot[...] = (jnp.broadcast_to(my_kind, (8, WIDE)) == eight).astype(F32)
        order = (eight + 1.0) * math.pi
        for ref in (dens0, dens1, ddens0, ddens1, summary, centre_acc, energy_acc):
            ref[...] = jnp.zeros_like(ref)

        def harmonics(k):
            return row(b, 0, k), [row(b, 1 + m, k) for m in range(3)]

        @pl.loop(0, NEIGH, unroll=UNROLL)
        def _(k):
            w, ys = harmonics(k)
            x = row(b, 4, k)
            scale = row(b, 5, k) / x
            basis = jnp.sin(order * x) * scale
            hot = (jnp.broadcast_to(row(b, 8, k), (8, WIDE)) == eight).astype(F32)
            inputs = jnp.concatenate([basis, kind_hot[...], hot, jnp.zeros_like(hot)], axis=0)
            half = mm(w_in[...], inputs.astype(BF16))
            value, slope = silu_parts(half)
            latent = value.astype(BF16)
            lat0[k] = latent
            slope0[k] = slope.astype(BF16)
            result = mm(w_first[...], latent)
            amp[k] = result[:64]
            half0[k] = result[64:]
            env = result[32:64] * (w * 0.25)
            dens0[0] += env
            for m in range(3):
                dens0[m + 1] += env * ys[m]

        @pl.loop(0, NEIGH, unroll=UNROLL)
        def _(k):
            w, ys = harmonics(k)
            a = amp[k, 0:32]
            d = [dens0[m] for m in range(4)]
            inner = d[1] * ys[0] + d[2] * ys[1] + d[3] * ys[2]
            pieces = [a * d[0], a * inner] + [a * (d[m + 1] + ys[m] * d[0]) for m in range(3)]
            joined = jnp.concatenate(pieces, axis=0).astype(BF16)
            result = mm(w_mix[...], joined)
            tens[k] = result[256:]
            value, slope = silu_parts(half0[k] + result[:256])
            slope1[k] = slope.astype(BF16)
            latent = (lat0[k].astype(F32) + value).astype(BF16)
            lat1[k] = latent
            result = mm(w_second[...], latent)
            envl[k] = result[:32]
            half1[k] = result[32:]
            env = result[:32] * (w * 0.25)
            dens1[0] += env
            for m in range(3):
                dens1[m + 1] += env * ys[m]

        @pl.loop(0, NEIGH, unroll=UNROLL)
        def _(k):
            w, ys = harmonics(k)
            t = [tens[k, 32 * m:32 * m + 32] for m in range(4)]
            d = [dens1[m] for m in range(4)]
            joined = jnp.concatenate(
                [t[0] * d[0], t[1] * d[1] + t[2] * d[2] + t[3] * d[3]], axis=0).astype(BF16)
            value, slope = silu_parts(half1[k] + mm(w_third[...], joined))
            latent = (lat1[k].astype(F32) + value).astype(BF16).astype(F32)
            summary[...] += latent * w
            weigh = w_energy[...]
            edge = jnp.sum(latent * weigh, axis=0, keepdims=True)
            back[k, 0:1] = edge
            energy_acc[...] += jnp.broadcast_to(edge * w, (8, WIDE))
            dl2 = weigh * w
            result = mm(b_second[...], (dl2 * slope).astype(BF16))
            dlat[k] = dl2 + result[:256]
            dscal[k] = result[256:]
            ddens1[0] += result[256:288] * t[0]
            for m in range(3):
                ddens1[m + 1] += result[288:320] * t[m + 1]

        @pl.loop(0, NEIGH, unroll=UNROLL)
        def _(k):
            w, ys = harmonics(k)
            q = [ddens1[m] * 0.25 for m in range(4)]
            env = envl[k]
            total = q[0] + q[1] * ys[0] + q[2] * ys[1] + q[3] * ys[2]
            dw = jnp.sum(env * total, axis=0, keepdims=True)
            env = env * w
            dy = [env * q[m + 1] for m in range(3)]
            da, db = dscal[k, 0:32], dscal[k, 32:64]
            pieces = [total * w, da * dens1[0]] + [db * dens1[m + 1] for m in range(3)]
            mixed = mm(b_mix[...], jnp.concatenate(pieces, axis=0).astype(BF16))
            dl1 = dlat[k] + mixed[:256]
            result = mm(b_first[...], (dl1 * slope1[k].astype(F32)).astype(BF16))
            dlat[k] = dl1 + result[:256]
            da = result[256:288] + mixed[256:288]
            db = result[288:320] + mixed[288:320]
            dv = [mixed[320 + 32 * m:352 + 32 * m] for m in range(3)]
            a = amp[k, 0:32]
            d = [dens0[m] for m in range(4)]
            inner = d[1] * ys[0] + d[2] * ys[1] + d[3] * ys[2]
            damp[k] = da * d[0] + db * inner + sum(dv[m] * (d[m + 1] + ys[m] * d[0]) for m in range(3))
            ba = db * a
            va = [dv[m] * a for m in range(3)]
            ddens0[0] += da * a + va[0] * ys[0] + va[1] * ys[1] + va[2] * ys[2]
            for m in range(3):
                ddens0[m + 1] += ba * ys[m] + va[m]
                dy[m] += ba * d[m + 1] + va[m] * d[0]
            back[k, 0:1] += dw
            for m in range(3):
                back[k, m + 1:m + 2] = jnp.sum(dy[m], axis=0, keepdims=True)

        @pl.loop(0, NEIGH, unroll=UNROLL)
        def _(k):
            w, ys = harmonics(k)
            q = [ddens0[m] * 0.25 for m in range(4)]
            env = amp[k, 32:64]
            total = q[0] + q[1] * ys[0] + q[2] * ys[1] + q[3] * ys[2]
            dw = back[k, 0:1] + jnp.sum(env * total, axis=0, keepdims=True)
            env = env * w
            dy = [back[k, m + 1:m + 2] + jnp.sum(env * q[m + 1], axis=0, keepdims=True) for m in range(3)]
            joined = jnp.concatenate([damp[k], total * w], axis=0).astype(BF16)
            dl0 = dlat[k] + mm(b_amp[...], joined)
            dbasis = mm(b_in[...], (dl0 * slope0[k].astype(F32)).astype(BF16))[:8]
            x, u, du, inv = row(b, 4, k), row(b, 5, k), row(b, 6, k), row(b, 7, k)
            ix = 1.0 / x
            angle = order * x
            slope = jnp.cos(angle) * order * (u * ix) + jnp.sin(angle) * ((du - u * ix) * ix)
            dx = jnp.sum(dbasis * slope, axis=0, keepdims=True) + dw * row(b, 10, k)
            dr = dx * row(b, 9, k)
            along = (ys[0] * dy[0] + ys[1] * dy[1] + ys[2] * dy[2]) * inv
            force = [ys[m] * (dr - along) + dy[m] * inv for m in range(3)]
            centre_acc[...] += jnp.concatenate(force + [jnp.zeros((5, WIDE), F32)], axis=0)
            index = near[pl.ds(k, 1), pl.ds(start, WIDE)]
            low = jnp.bitwise_and(index, LANES - 1)
            high = jnp.right_shift(index, 7)
            picker = (lax.broadcasted_iota(jnp.int32, (LANES, WIDE), 0) == low).astype(F32).astype(BF16)
            places = lax.broadcasted_iota(jnp.int32, (16, WIDE), 0) == high
            spread = [jnp.where(places, f, 0.0) for f in force]
            spread = jnp.concatenate(spread, axis=0)
            top = spread.astype(BF16)
            rest = (spread - top.astype(F32)).astype(BF16)
            both = jnp.concatenate([top, rest], axis=0)
            ghost_acc[...] += lax.dot_general(
                both, picker, (((1,), (1,)), ((), ())), preferred_element_type=F32)

        lanes = pl.ds(start, WIDE)
        grad_out[:, lanes] = -centre_acc[...]
        energy_out[:, lanes] = energy_acc[...]
        feature_out[0:256, lanes] = summary[...] * 0.25
        for m in range(4):
            feature_out[256 + 32 * m:288 + 32 * m, lanes] = dens1[m]

    grad_out[:, slots:] = jnp.zeros_like(grad_out[:, slots:])
    for c in range(3):
        for h in range(sub):
            lanes = slice(h * LANES, (h + 1) * LANES)
            grad_out[c:c + 1, lanes] += (
                ghost_acc[16 * c + h:16 * c + h + 1] + ghost_acc[48 + 16 * c + h:49 + 16 * c + h])


def evaluate(ext, near, embed_weight, tensor_weight, env_weight, scalar_mix, vector_mix, latent_weight, energy_weight):
    slots = near.shape[1]
    blocks = slots // WIDE
    v = lambda shape, dtype=F32: pltpu.VMEM(shape, dtype)
    scratch = [
        v((256, 32), BF16), v((320, 256), BF16), v((384, 160), BF16), v((288, 256), BF16), v((256, 64), BF16),
        v((256, WIDE)), v((320, 256), BF16), v((416, 160), BF16), v((320, 256), BF16), v((256, 64), BF16),
        v((16, 256), BF16), v((256, 128)),
        v((blocks, 11, NEIGH, WIDE)), v((8, WIDE)),
        v((NEIGH, 256, WIDE), BF16), v((NEIGH, 256, WIDE), BF16), v((NEIGH, 256, WIDE)),
        v((NEIGH, 64, WIDE)), v((NEIGH, 128, WIDE)), v((NEIGH, 32, WIDE)),
        v((NEIGH, 256, WIDE), BF16), v((NEIGH, 256, WIDE), BF16), v((NEIGH, 256, WIDE)),
        v((NEIGH, 256, WIDE)), v((NEIGH, 64, WIDE)), v((NEIGH, 32, WIDE)), v((NEIGH, 8, WIDE)),
        v((4, 32, WIDE)), v((4, 32, WIDE)), v((4, 32, WIDE)), v((4, 32, WIDE)),
        v((256, WIDE)), v((96, LANES)), v((8, WIDE)), v((8, WIDE)),
    ]
    return pl.pallas_call(
        force_kernel,
        out_shape=(
            jax.ShapeDtypeStruct(ext.shape, F32),
            jax.ShapeDtypeStruct((8, slots), F32),
            jax.ShapeDtypeStruct((384, slots), F32),
        ),
        in_specs=[pl.BlockSpec(memory_space=pltpu.VMEM)] * 9,
        out_specs=[pl.BlockSpec(memory_space=pltpu.VMEM)] * 3,
        scratch_shapes=scratch,
        compiler_params=pltpu.CompilerParams(vmem_limit_bytes=56 * 1024 * 1024),
    )(ext, near, embed_weight, tensor_weight, env_weight, scalar_mix, vector_mix, latent_weight, energy_weight[None])


MESH = pl.DeviceIdType.MESH
EXACT_PARTS = 3


def parts_of(value, count):
    found = []
    for _ in range(count):
        piece = value.astype(BF16)
        found.append(piece)
        value = value - piece.astype(F32)
    return found


def tn(a, b):
    return lax.dot_general(a, b, (((0,), (0,)), ((), ())), preferred_element_type=F32)


def nt(a, b):
    return lax.dot_general(a, b, (((1,), (1,)), ((), ())), preferred_element_type=F32)


def partners():
    slab, dom = lax.axis_index("slab"), lax.axis_index("dom")
    slabs, doms = lax.axis_size("slab"), lax.axis_size("dom")
    linear = slab * doms + dom
    after = lax.rem(linear + 1, slabs * doms)
    before = lax.rem(linear + slabs * doms - 1, slabs * doms)
    split = lambda index: (index // doms, lax.rem(index, doms))
    return slab, dom, doms, split(before), split(after)


def greet(slab, dom, doms, before, after):
    barrier = pltpu.get_barrier_semaphore()

    @pl.loop(1, doms)
    def _(step):
        pl.semaphore_signal(
            barrier, inc=1, device_id=(slab, lax.rem(dom + step, doms)), device_id_type=MESH)

    for other in (before, after):
        pl.semaphore_signal(barrier, inc=1, device_id=other, device_id_type=MESH)
    return barrier


def send(source, target, send_sem, recv_sem, device):
    copy = pltpu.make_async_remote_copy(
        src_ref=source, dst_ref=target, send_sem=send_sem, recv_sem=recv_sem,
        device_id=device, device_id_type=MESH)
    copy.start()
    return copy


def reordered(slot):
    source = jnp.right_shift(slot * 43691, 19)
    return (slot - 12 * source) * 64 + source


def front_kernel(
    positions, species, domain, neighbours, ghost_lists,
    ext_out, near_out, code_out, lists_out,
    outbox, inbox, square, lend, arrive, box_send, box_recv, ghost_send, ghost_recv,
):
    slab, dom, doms, before, after = partners()
    barrier = greet(slab, dom, doms, before, after)
    atoms = positions.shape[1]
    slots = neighbours.shape[1]
    ghosts = ghost_lists.shape[1]

    target = domain[...]
    hot = (lax.broadcasted_iota(jnp.int32, (atoms, doms), 1) == target).astype(F32)
    hot16 = hot.astype(BF16)
    lower = (lax.broadcasted_iota(jnp.int32, (atoms, atoms), 0)
             > lax.broadcasted_iota(jnp.int32, (atoms, atoms), 1)).astype(F32).astype(BF16)
    rank = jnp.sum(hot * mm(lower, hot16), axis=1, keepdims=True)
    values = jnp.concatenate(
        [positions[...], species[...].astype(F32) + 1.0, jnp.zeros((4, atoms), F32)], axis=0).T
    lane = lax.broadcasted_iota(jnp.int32, (atoms, LANES), 1)
    lane_rank = jnp.bitwise_and(lane, 15).astype(F32)
    lane_comp = jnp.right_shift(lane, 4)
    packed = jnp.zeros((atoms, LANES), F32)
    for c in range(4):
        packed = jnp.where((lane_comp == c) & (lane_rank == rank), values[:, c:c + 1], packed)
    message = sum(tn(hot16, piece) for piece in parts_of(packed, EXACT_PARTS))
    for d in range(64):
        outbox[d] = message[d:d + 1]
    inbox[dom] = outbox[dom]

    pl.semaphore_wait(barrier, doms + 1)

    @pl.loop(1, doms)
    def _(step):
        other = lax.rem(dom + step, doms)
        send(outbox.at[other], inbox.at[dom], box_send, box_recv, (slab, other))

    code = jnp.where(lane == 0, target.astype(F32), jnp.where(lane == 1, rank, 0.0))
    code_out[...] = code.T[:8]
    index = neighbours[...]
    pieces = jnp.concatenate(
        [jnp.right_shift(index, 7).astype(F32), jnp.bitwise_and(index, LANES - 1).astype(F32)], axis=0)
    place = lax.broadcasted_iota(jnp.int32, (slots, slots), 1)
    place = jnp.bitwise_and(place, 63) * 12 + jnp.right_shift(place, 6)
    mover = (lax.broadcasted_iota(jnp.int32, (slots, slots), 0) == place).astype(F32).astype(BF16)
    moved = mm(pieces.astype(BF16), mover).astype(jnp.int32)
    index = moved[:16] * LANES + moved[16:]
    near_out[...] = jnp.where(index < slots, reordered(index), index)
    lists = reordered(ghost_lists[...])
    lists_out[...] = lists
    rows = lax.broadcasted_iota(jnp.int32, (slots, ghosts), 0)
    picks = [(rows == lists[i:i + 1]).astype(F32).astype(BF16) for i in range(2)]

    arrived = pltpu.make_async_copy(inbox.at[pl.ds(0, 63)], inbox.at[pl.ds(0, 63)], box_recv)
    arrived.wait()
    square[...] = jnp.zeros_like(square)
    for s in range(64):
        square[s:s + 1] = inbox[s]
    turned = square[...].T
    rolled = pltpu.roll(turned, 64, 1)
    first = lax.broadcasted_iota(jnp.int32, (1, LANES), 1) < 64
    ext_out[4:8, 0:slots] = jnp.zeros((4, slots), F32)
    for c in range(4):
        for p in range(slots // LANES):
            even = turned[16 * c + 2 * p:16 * c + 2 * p + 1]
            odd = rolled[16 * c + 2 * p + 1:16 * c + 2 * p + 2]
            both = jnp.where(first, even, odd)
            ext_out[c:c + 1, p * LANES:(p + 1) * LANES] = both - 1.0 if c == 3 else both
    own = parts_of(ext_out[:, 0:slots], EXACT_PARTS)
    copies = []
    for i, other in ((0, before), (1, after)):
        lend[i] = sum(mm(piece, picks[i]) for piece in own)
        copies.append(send(lend.at[i], arrive.at[i], ghost_send.at[i], ghost_recv.at[i], other))
    pltpu.make_async_copy(outbox.at[pl.ds(0, 63)], outbox.at[pl.ds(0, 63)], box_send).wait()
    for copy in copies:
        copy.wait()
    ext_out[:, slots:slots + ghosts] = arrive[1]
    ext_out[:, slots + ghosts:] = arrive[0]


def front(positions, species, domain, neighbours, ghost_lists):
    slots, ghosts, atoms = neighbours.shape[1], ghost_lists.shape[1], positions.shape[1]
    v = lambda shape, dtype=F32: pltpu.VMEM(shape, dtype)
    dma = pltpu.SemaphoreType.DMA
    return pl.pallas_call(
        front_kernel,
        out_shape=(
            jax.ShapeDtypeStruct((8, 2 * slots), F32),
            jax.ShapeDtypeStruct((NEIGH, slots), jnp.int32),
            jax.ShapeDtypeStruct((8, atoms), F32),
            jax.ShapeDtypeStruct((2, ghosts), jnp.int32),
        ),
        in_specs=[pl.BlockSpec(memory_space=pltpu.VMEM)] * 5,
        out_specs=[pl.BlockSpec(memory_space=pltpu.VMEM)] * 4,
        scratch_shapes=[
            v((64, 1, LANES)), v((64, 1, LANES)), v((LANES, LANES)), v((2, 8, ghosts)), v((2, 8, ghosts)),
            dma, dma, dma((2,)), dma((2,)),
        ],
        compiler_params=pltpu.CompilerParams(
            collective_id=0, has_side_effects=True, vmem_limit_bytes=32 * 1024 * 1024),
    )(positions, species[None], domain, neighbours, ghost_lists)


ROWS = 40


def home_kernel(
    grad, energy, features, code, lists,
    force_out, energy_out, feature_out,
    outbox, inbox, back, square, box_send, box_recv, ghost_send, ghost_recv,
):
    slab, dom, doms, before, after = partners()
    barrier = greet(slab, dom, doms, before, after)
    slots, ghosts = energy.shape[1], lists.shape[1]
    atoms = code.shape[1]
    pl.semaphore_wait(barrier, doms + 1)
    copies = [
        send(grad.at[:, pl.ds(slots, ghosts)], back.at[0], ghost_send.at[0], ghost_recv.at[0], before),
        send(grad.at[:, pl.ds(slots + ghosts, ghosts)], back.at[1], ghost_send.at[1], ghost_recv.at[1], after),
    ]
    for p in range(slots // LANES):
        turned = features[:, p * LANES:(p + 1) * LANES].T
        for i in range(LANES // 8):
            place = p * LANES + 8 * i
            r, d = place // 64, place % 64
            for t in range(3):
                outbox[pl.ds(ROWS * d + 3 * r + t, 8, stride=ROWS), :] = (
                    turned[8 * i:8 * i + 8, t * LANES:(t + 1) * LANES])
    for copy in copies:
        copy.wait()
    columns = lax.broadcasted_iota(jnp.int32, (slots, ghosts), 0)
    total = grad[:, 0:slots]
    for i in range(2):
        hot = (columns == lists[1 - i:2 - i]).astype(F32).astype(BF16)
        total = total + sum(nt(piece, hot) for piece in parts_of(back[i], 2))
    square[...] = jnp.zeros_like(square)
    rows = [-total[c:c + 1] for c in range(3)] + [energy[0:1]]
    for c in range(4):
        for p in range(slots // LANES):
            piece = rows[c][:, p * LANES:(p + 1) * LANES]
            square[16 * c + 2 * p:16 * c + 2 * p + 1] = piece
            square[16 * c + 2 * p + 1:16 * c + 2 * p + 2] = pltpu.roll(piece, 64, 1)
    turned = square[...].T
    for i in range(8):
        outbox[pl.ds(ROWS * 8 * i + 36, 8, stride=ROWS), :] = turned[8 * i:8 * i + 8]
        for t in range(37, ROWS):
            outbox[pl.ds(ROWS * 8 * i + t, 8, stride=ROWS), :] = jnp.zeros((8, LANES), F32)

    @pl.loop(1, doms)
    def _(step):
        other = lax.rem(dom + step, doms)
        send(outbox.at[pl.ds(pl.multiple_of(other * ROWS, 8), ROWS)],
             inbox.at[pl.ds(pl.multiple_of(dom * ROWS, 8), ROWS)], box_send, box_recv, (slab, other))

    mine = pl.ds(pl.multiple_of(dom * ROWS, 8), ROWS)
    inbox[mine] = outbox[mine]
    target, rank = code[0:1], code[1:2]
    hot = (lax.broadcasted_iota(jnp.int32, (64, atoms), 0).astype(F32) == target).astype(F32)
    hots = jnp.concatenate([jnp.where(rank == float(r), hot, 0.0).astype(BF16) for r in range(12)], axis=0)
    most = pl.ds(0, 63 * ROWS)
    pltpu.make_async_copy(inbox.at[most], inbox.at[most], box_recv).wait()
    pltpu.make_async_copy(outbox.at[most], outbox.at[most], box_send).wait()
    for t in range(3):
        found = jnp.concatenate([inbox[pl.ds(3 * r + t, 64, stride=ROWS), :] for r in range(12)], axis=0)
        feature_out[t * LANES:(t + 1) * LANES] = sum(tn(piece, hots) for piece in parts_of(found, 2))
    found = inbox[pl.ds(36, 64, stride=ROWS), :]
    picked = sum(tn(piece, hot.astype(BF16)) for piece in parts_of(found, 2))
    right = (lax.broadcasted_iota(jnp.int32, (16, atoms), 0).astype(F32) == rank).astype(F32)
    result = [jnp.sum(picked[16 * c:16 * c + 16] * right, axis=0, keepdims=True) for c in range(4)]
    for c in range(3):
        force_out[c:c + 1] = result[c]
    energy_out[...] = result[3]


def home(grad, energy, features, code, lists):
    atoms, ghosts = code.shape[1], lists.shape[1]
    v = lambda shape, dtype=F32: pltpu.VMEM(shape, dtype)
    dma = pltpu.SemaphoreType.DMA
    return pl.pallas_call(
        home_kernel,
        out_shape=(
            jax.ShapeDtypeStruct((3, atoms), F32),
            jax.ShapeDtypeStruct((1, atoms), F32),
            jax.ShapeDtypeStruct((384, atoms), F32),
        ),
        in_specs=[pl.BlockSpec(memory_space=pltpu.VMEM)] * 5,
        out_specs=[pl.BlockSpec(memory_space=pltpu.VMEM)] * 3,
        scratch_shapes=[
            v((64 * ROWS, LANES)), v((64 * ROWS, LANES)), v((2, 8, ghosts)), v((LANES, LANES)),
            dma, dma, dma((2,)), dma((2,)),
        ],
        compiler_params=pltpu.CompilerParams(
            collective_id=1, has_side_effects=True, vmem_limit_bytes=32 * 1024 * 1024),
    )(grad, energy, features, code, lists)


def local(
    positions, species, domain, neighbours, ghost_lists,
    embed_weight, tensor_weight, env_weight, scalar_mix, vector_mix, latent_weight, energy_weight,
):
    ext, near, code, lists = front(positions, species, domain, neighbours, ghost_lists)
    grad, energy, features = evaluate(
        ext, near, embed_weight, tensor_weight, env_weight, scalar_mix, vector_mix, latent_weight, energy_weight)
    forces, atom_energy, atom_features = home(grad, energy, features, code, lists)
    return forces, atom_energy[0], atom_features


def solution(mesh):
    both = ("slab", "dom")
    in_specs = (P(None, both), P(both), P(both, None), P(None, both), P(None, both)) + (P(),) * 7
    out_specs = (P(None, both), P(both), P(None, both))
    return jax.shard_map(local, mesh=mesh, in_specs=in_specs, out_specs=out_specs, check_vma=False)
```

time: 479 us -> 142 us (0.30)
  matrix products: 191 us -> 0 us
  Pallas kernels: 0 us -> 123 us
  local copies, waits for them, and re-layouts: 97.3 us -> 14.7 us
  other arithmetic: 72.8 us -> 0.6 us
  waiting for transfers between devices: 60.8 us -> 0 us
  starting transfers between devices: 39.1 us -> 0 us
  loops' own time: 10.2 us -> 0 us
    dot_general x116 -> x0, matrix products: 191 us -> none  [the longest x12 61.5 us: block_terms(): jnp.dot(stacked, picker, precision=exact)]
    pallas_call x0 -> x3, Pallas kernels: none -> 123 us  [the longest x1 62.8 us: evaluate(): pl.pallas_call(force_kernel, out_shape=(jax.ShapeDtypeStruct(ext.shape, F...]
    all_to_all x3 -> x0, waiting for transfers between devices: 58.3 us -> none  [the longest x1 37.9 us: local(): lax.all_to_all(feature_cols, 'dom', split_axis=1, concat_axis=1, tiled=True)]
    while x774 -> x0, local copies, waits for them, and re-layouts: 37.1 us -> none
    all_to_all x3 -> x0, starting transfers between devices: 29.3 us -> none  [the longest x1 13.2 us: local(): lax.all_to_all(outgoing, 'dom', split_axis=1, concat_axis=1, tiled=True)]
    reduce_sum x91 -> x0, other arithmetic: 27.6 us -> none  [the longest x12 12.9 us: block_terms(): env_edge = harmonics[:, :, None] * env_amp[:, None, :]]
    reshape x18 -> x0, local copies, waits for them, and re-layouts: 19.1 us -> none  [the longest x12 16.6 us: block_terms(): spread = spread.reshape(edge_count, 4, chan_count)]
    mul x66 -> x0, other arithmetic: 13.9 us -> none  [the longest x6 6.48 us: block_terms(): tensor[:, 1:] * spread[:, 1:]]
  transfers between devices with their start and end apart: 7 -> 0, of which waited for: 5 -> 0; matrix products, arithmetic and copies ran while one was open for 1% -> 0% of each run, Pallas kernels for 0% -> 0%
where the time goes in v1:
time: 142 us; the launch traced here: 139 us
  Pallas kernels  123 us (87%)
  local copies, waits for them, and re-layouts  14.7 us (10%)
    pallas_call x1, Pallas kernels, evaluate(): pl.pallas_call(force_kernel, out_shape=(jax.ShapeDtypeStruct(ext.shape, F...  62.8 us
    pallas_call x1, Pallas kernels, home(): pl.pallas_call(home_kernel, out_shape=(jax.ShapeDtypeStruct((3, atoms), F...  42.3 us
    pallas_call x1, Pallas kernels, front(): pl.pallas_call(front_kernel, out_shape=(jax.ShapeDtypeStruct((8, 2 * slot...  18.4 us
    unnamed x22, local copies, waits for them, and re-layouts  12.8 us

profile of v1, /device:TPU:1, one launch (start us, length us, event | category | flops | bytes accessed | tf_op | source)
XLA Modules:
  0.0 139.4 jit_solution(941663817344702770)
XLA Ops:
  0.6 1.2 broadcast_in_dim.7.energy_weight
  1.9 0.7 broadcast_in_dim.6.species
  2.5 1.4 %copy.18.scalar_mix = f32[64,32]{1,0:T(8,128)} copy(f32[64,32]{0,1:T(8,128)} %param.20) | data formatting | bytes 16384 | tf_op args[8]
  3.9 1.4 %copy.16.tensor_weight = bf16[256,32]{1,0:T(8,128)(2,1)} copy(bf16[256,32]{0,1:T(8,128)(2,1)} %param.18) | data formatting | bytes 32768 | tf_op args[6]
  5.4 1.5 %copy.17.env_weight = bf16[2,256,32]{2,1,0:T(8,128)(2,1)} copy(bf16[2,256,32]{1,2,0:T(8,128)(2,1)} %param.19) | data formatting | bytes 65536 | tf_op args[7]
  6.9 0.8 copy.15.domain
  7.7 0.0 copy-start.2
  7.7 0.8 copy-done.2
  8.5 0.0 copy-start.6
  8.5 0.7 copy-done.6
  9.2 0.0 copy-start.7
  9.2 0.7 copy-done.7
  9.9 18.4 %shard_map.139 = (f32[8,1536]{1,0:T(8,128)S(1)}, s32[16,768]{1,0:T(8,128)S(1)}, f32[8,384]{1,0:T(8,128)S(1)}, s32[2,384]{1,0:T(2,128)S(1)}) custom-call(f32[3,384]{1,0:T(4,128)S(1)} %copy-done.6, s32[1,384]{1,0:T(1,128)S(1)} %broadcast_in_dim.6.species, s32[384,1]{1,0:T(8,128)S(1)} %copy.15.domain, s32[16,768]{1,0:T(8,128)S(1)} %copy-done.2, ...), custom_call_target="tpu_custom_call" | custom-call | tf_op jit(solution)/shard_map/pallas_call | solution.py:450
  28.3 0.0 copy-start.3
  28.3 0.6 copy-done.3
  28.9 0.0 copy-start.4
  28.9 0.6 copy-done.4
  29.5 62.8 %shard_map.140 = (f32[8,1536]{1,0:T(8,128)}, f32[8,768]{1,0:T(8,128)}, f32[384,768]{1,0:T(8,128)}) custom-call(f32[8,1536]{1,0:T(8,128)} %copy-done.3, s32[16,768]{1,0:T(8,128)} %copy-done.4, bf16[24,256]{1,0:T(8,128)(2,1)} %embed_weight.1, bf16[256,32]{1,0:T(8,128)(2,1)} %copy.16.tensor_weight, bf16[2,256,32]{2,1,0:T(8,128)(2,1)} %copy.17.env_weight, ...), custom_call_target="tpu_custom_call" | custom-call | tf_op jit(solution)/shard_map/pallas_call | solution.py:295
  92.3 0.0 copy-start
  92.3 1.3 copy-done
  93.6 0.0 copy-start.1
  93.6 0.8 copy-done.1
  94.4 0.0 copy-start.5
  94.4 0.7 copy-done.5
  95.2 42.3 %shard_map.141 = (f32[3,384]{1,0:T(4,128)S(1)}, f32[1,384]{1,0:T(1,128)S(1)}, f32[384,384]{1,0:T(8,128)S(1)}) custom-call(f32[8,1536]{1,0:T(8,128)S(1)} %copy-done.1, f32[8,768]{1,0:T(8,128)S(1)} %copy-done.5, f32[384,768]{1,0:T(8,128)S(1)} %copy-done, f32[8,384]{1,0:T(8,128)S(1)} %get-tuple-element.18.code, s32[2,384]{1,0:T(2,128)S(1)} %get-tuple-element.19.lists), custom_call_target="tpu_custom_call" | custom-call | tf_op jit(solution)/shard_map/pallas_call | solution.py:544
  137.4 0.6 reduce
  138.0 0.6 copy.21
  138.6 0.8 copy.22
Async XLA Ops:
  7.7 0.8 copy-start.2
  8.5 0.7 copy-start.6
  9.2 0.7 copy-start.7
  28.3 0.6 copy-start.3
  28.9 0.6 copy-start.4
  92.3 1.3 copy-start
  93.6 0.8 copy-start.1
  94.4 0.7 copy-start.5

commit v2 on v1

v2 whole, which is shorter than its diff:
```python
import math

import jax
import jax.numpy as jnp
from jax import lax
from jax.experimental import pallas as pl
from jax.experimental.pallas import tpu as pltpu
from jax.sharding import PartitionSpec as P

F32 = jnp.float32
BF16 = jnp.bfloat16
LANES = 128
WIDE = 256
NEIGH = 16
UNROLL = 4
MESH = pl.DeviceIdType.MESH
EXACT_PARTS = 3
RANKS = 12
EARLY = 24
LATE = 16


def mm(a, b):
    return jnp.dot(a, b, preferred_element_type=F32)


def silu_parts(half):
    gate = jnp.tanh(half)
    rise = 1.0 + gate
    value = half * rise
    slope = rise + value * (1.0 - gate)
    return value, slope


def parts_of(value, count):
    found = []
    for _ in range(count):
        piece = value.astype(BF16)
        found.append(piece)
        value = value - piece.astype(F32)
    return found


def tn(a, b):
    return lax.dot_general(a, b, (((0,), (0,)), ((), ())), preferred_element_type=F32)


def nt(a, b):
    return lax.dot_general(a, b, (((1,), (1,)), ((), ())), preferred_element_type=F32)


def partners():
    slab, dom = lax.axis_index("slab"), lax.axis_index("dom")
    slabs, doms = lax.axis_size("slab"), lax.axis_size("dom")
    linear = slab * doms + dom
    after = lax.rem(linear + 1, slabs * doms)
    before = lax.rem(linear + slabs * doms - 1, slabs * doms)
    split = lambda index: (index // doms, lax.rem(index, doms))
    return slab, dom, doms, split(before), split(after)


def greet(slab, dom, doms, before, after):
    barrier = pltpu.get_barrier_semaphore()

    @pl.loop(1, doms)
    def _(step):
        pl.semaphore_signal(
            barrier, inc=1, device_id=(slab, lax.rem(dom + step, doms)), device_id_type=MESH)

    for other in (before, after):
        pl.semaphore_signal(barrier, inc=1, device_id=other, device_id_type=MESH)
    return barrier


def send(source, target, send_sem, recv_sem, device):
    copy = pltpu.make_async_remote_copy(
        src_ref=source, dst_ref=target, send_sem=send_sem, recv_sem=recv_sem,
        device_id=device, device_id_type=MESH)
    copy.start()
    return copy


def reordered(slot):
    source = jnp.right_shift(slot * 43691, 19)
    return (slot - 12 * source) * 64 + source


def arrange_weights(
    embed_weight, tensor_turned, env_turned, scalar_turned, vector_mix, latent_weight, energy_weight,
    w_in, w_first, w_mix, w_second, w_third, w_energy, b_second, b_mix, b_first, b_amp, b_in, stage,
):
    chan, width = tensor_turned.shape
    lat0, lat1 = latent_weight[0].astype(F32) * 0.5, latent_weight[1].astype(F32) * 0.5
    b_first[...] = lat0.astype(BF16)
    b_second[...] = lat1.astype(BF16)
    w_first[0:32] = tensor_turned[...]
    w_first[32:64] = env_turned[0]
    w_second[0:32] = env_turned[1]
    small = jnp.concatenate(
        [tensor_turned[...], env_turned[0], env_turned[1], jnp.zeros((chan, width), BF16)], axis=0)
    small = small.astype(F32).T.astype(BF16)
    b_amp[...] = small[:, :64]
    w_first[64:] = lat0[:width].T.astype(BF16)
    w_second[32:] = lat1[:width].T.astype(BF16)
    w_third[...] = lat1[width:].T.astype(BF16)
    embed = embed_weight[...].astype(F32) * 0.5
    b_in[...] = embed[:16].astype(BF16)
    w_in[...] = jnp.concatenate([embed, jnp.zeros((8, width), F32)], axis=0).T.astype(BF16)
    energy = jnp.broadcast_to(energy_weight[...].astype(F32).reshape(1, width), (8, width))
    w_energy[...] = energy.T[:, 0:1] + jnp.zeros((width, WIDE), F32)
    stage[...] = jnp.zeros_like(stage)
    stage[0:32, 0:32] = vector_mix[...]
    turned = stage[:, 0:LANES].T[0:32, 0:32]
    stage[0:32, 0:64] = scalar_turned[...]
    for m in range(3):
        stage[32 + 32 * m:64 + 32 * m, 64 + 32 * m:96 + 32 * m] = turned
    core = stage[...]
    b_mix[...] = jnp.zeros_like(b_mix)
    b_mix[0:width, 0:32] = small[:, 64:96]
    b_mix[width:, 32:] = core.T[0:160].astype(BF16)
    w_mix[...] = jnp.zeros_like(w_mix)
    w_mix[0:width, 0:64] = lat0[width:].T.astype(BF16)
    w_mix[width:] = core[:, 0:160].astype(BF16)


def whole_kernel(
    positions, species, domain, neighbours, ghost_lists,
    embed_weight, tensor_turned, env_turned, scalar_turned, vector_mix, latent_weight, energy_weight,
    force_out, energy_out, feature_out,
    outbox, inbox, square, lend, arrive, box_send, box_recv, ghost_send, ghost_recv,
    ext, near, picks, home_hot, home_hots, home_rank, flipped, grad, energies, back_in,
    early_out, early_in, late_out, late_in, force_box, force_in,
    early_send, early_recv, late_send, late_recv, force_send, force_recv, back_send, back_recv,
    w_in, w_first, w_mix, w_second, w_third, w_energy, b_second, b_mix, b_first, b_amp, b_in, stage,
    geo, kind_hot, lat0, slope0, half0, amp, tens, envl, lat1, slope1, half1, dlat, dscal, damp, back,
    dens0, dens1, ddens0, ddens1, summary, ghost_acc, centre_acc, energy_acc,
):
    slab, dom, doms, before, after = partners()
    barrier = greet(slab, dom, doms, before, after)
    atoms = positions.shape[1]
    slots = neighbours.shape[1]
    ghosts = ghost_lists.shape[1]

    spread = jnp.broadcast_to(domain[...].astype(F32), (8, atoms))
    target = spread.T[:, 0:1].astype(jnp.int32)
    hot = (lax.broadcasted_iota(jnp.int32, (atoms, doms), 1) == target).astype(F32)
    hot16 = hot.astype(BF16)
    lower = (lax.broadcasted_iota(jnp.int32, (atoms, atoms), 0)
             > lax.broadcasted_iota(jnp.int32, (atoms, atoms), 1)).astype(F32).astype(BF16)
    rank = jnp.sum(hot * mm(lower, hot16), axis=1, keepdims=True)
    values = jnp.concatenate(
        [positions[...], species[...].astype(F32).reshape(1, atoms) + 1.0, jnp.zeros((4, atoms), F32)], axis=0).T
    lane = lax.broadcasted_iota(jnp.int32, (atoms, LANES), 1)
    lane_rank = jnp.bitwise_and(lane, 15).astype(F32)
    lane_comp = jnp.right_shift(lane, 4)
    packed = jnp.zeros((atoms, LANES), F32)
    for c in range(4):
        packed = jnp.where((lane_comp == c) & (lane_rank == rank), values[:, c:c + 1], packed)
    message = sum(tn(hot16, piece) for piece in parts_of(packed, EXACT_PARTS))
    for d in range(64):
        outbox[d] = message[d:d + 1]
    inbox[dom] = outbox[dom]

    pl.semaphore_wait(barrier, doms + 1)

    @pl.loop(1, doms)
    def _(step):
        other = lax.rem(dom + step, doms)
        send(outbox.at[other], inbox.at[dom], box_send, box_recv, (slab, other))

    code = jnp.where(lane == 0, target.astype(F32), jnp.where(lane == 1, rank, 0.0))
    code = code.T
    target, rank = code[0:1], code[1:2]
    hot = (lax.broadcasted_iota(jnp.int32, (64, atoms), 0).astype(F32) == target).astype(F32)
    home_hot[...] = hot.astype(BF16)
    for r in range(RANKS):
        home_hots[64 * r:64 * r + 64] = jnp.where(rank == float(r), hot, 0.0).astype(BF16)
    home_rank[...] = (lax.broadcasted_iota(jnp.int32, (16, atoms), 0).astype(F32) == rank).astype(F32)
    arrange_weights(
        embed_weight, tensor_turned, env_turned, scalar_turned, vector_mix, latent_weight, energy_weight,
        w_in, w_first, w_mix, w_second, w_third, w_energy, b_second, b_mix, b_first, b_amp, b_in, stage)
    index = neighbours[...]
    pieces = jnp.concatenate(
        [jnp.right_shift(index, 7).astype(F32), jnp.bitwise_and(index, LANES - 1).astype(F32)], axis=0)
    place = lax.broadcasted_iota(jnp.int32, (slots, slots), 1)
    place = jnp.bitwise_and(place, 63) * 12 + jnp.right_shift(place, 6)
    mover = (lax.broadcasted_iota(jnp.int32, (slots, slots), 0) == place).astype(F32).astype(BF16)
    moved = mm(pieces.astype(BF16), mover).astype(jnp.int32)
    index = moved[:16] * LANES + moved[16:]
    near[...] = jnp.where(index < slots, reordered(index), index)
    lists = reordered(ghost_lists[...])
    rows = lax.broadcasted_iota(jnp.int32, (slots, ghosts), 0)
    for i in range(2):
        picks[i] = (rows == lists[i:i + 1]).astype(F32).astype(BF16)

    arrived = pltpu.make_async_copy(inbox.at[pl.ds(0, 63)], inbox.at[pl.ds(0, 63)], box_recv)
    arrived.wait()
    square[...] = jnp.zeros_like(square)
    for s in range(64):
        square[s:s + 1] = inbox[s]
    turned = square[...].T
    rolled = pltpu.roll(turned, 64, 1)
    first = lax.broadcasted_iota(jnp.int32, (1, LANES), 1) < 64
    ext[4:8, 0:slots] = jnp.zeros((4, slots), F32)
    for c in range(4):
        for p in range(slots // LANES):
            even = turned[16 * c + 2 * p:16 * c + 2 * p + 1]
            odd = rolled[16 * c + 2 * p + 1:16 * c + 2 * p + 2]
            both = jnp.where(first, even, odd)
            ext[c:c + 1, p * LANES:(p + 1) * LANES] = both - 1.0 if c == 3 else both
    own = parts_of(ext[:, 0:slots], EXACT_PARTS)
    copies = []
    for i, other in ((0, before), (1, after)):
        lend[i] = sum(mm(piece, picks[i]) for piece in own)
        copies.append(send(lend.at[i], arrive.at[i], ghost_send.at[i], ghost_recv.at[i], other))
    pltpu.make_async_copy(outbox.at[pl.ds(0, 63)], outbox.at[pl.ds(0, 63)], box_send).wait()
    for copy in copies:
        copy.wait()
    ext[:, slots:slots + ghosts] = arrive[1]
    ext[:, slots + ghosts:] = arrive[0]
    blocks = geo.shape[0]
    sub = ext.shape[1] // LANES
    own = ext
    ghost_acc[...] = jnp.zeros_like(ghost_acc)

    for piece in range(blocks * WIDE // LANES):
        b, half = piece // 2, piece % 2
        lanes = pl.ds(half * LANES, LANES)
        index = near[:, piece * LANES:(piece + 1) * LANES]
        low = jnp.bitwise_and(index, LANES - 1)
        high = jnp.right_shift(index, 7)
        got = []
        for comp in range(4):
            value = jnp.zeros((NEIGH, LANES), F32)
            for h in range(sub):
                row = jnp.broadcast_to(ext[comp:comp + 1, h * LANES:(h + 1) * LANES], (NEIGH, LANES))
                taken = jnp.take_along_axis(row, low, axis=1)
                value = jnp.where(high == h, taken, value)
            got.append(value)
        mine = [own[c:c + 1, piece * LANES:(piece + 1) * LANES] for c in range(4)]
        off = [got[c] - mine[c] for c in range(3)]
        radius = jnp.sqrt(off[0] * off[0] + off[1] * off[1] + off[2] * off[2] + 0.25)
        inv = 1.0 / radius
        x = jnp.minimum(radius * 0.2, 1.0)
        x2 = x * x
        x3 = x2 * x
        x5 = x2 * x3
        u = 1.0 + x3 * x3 * (-28.0 + x * (48.0 - 21.0 * x))
        du = -168.0 * x5 * (1.0 - x) * (1.0 - x)
        du = jnp.where(radius < 5.0, du, 0.0)
        slot = piece * LANES + lax.broadcasted_iota(jnp.int32, (NEIGH, LANES), 1)
        live = (mine[3] >= 0.0) & (got[3] >= 0.0) & (index != slot)
        w = jnp.where(live, u, 0.0)
        items = [w, off[0] * inv, off[1] * inv, off[2] * inv, x, u, du, inv, got[3],
                 jnp.where(radius < 5.0, 0.2, 0.0), jnp.where(live, du, 0.0)]
        for c, item in enumerate(items):
            geo[b, c, :, lanes] = item

    def row(b, c, k):
        return geo[b, c, pl.ds(k, 1), :]

    @pl.loop(0, blocks)
    def _(b):
        start = pl.multiple_of(b * WIDE, WIDE)
        eight = lax.broadcasted_iota(jnp.int32, (8, WIDE), 0).astype(F32)
        my_kind = own[3:4, pl.ds(start, WIDE)]
        kind_hot[...] = (jnp.broadcast_to(my_kind, (8, WIDE)) == eight).astype(F32)
        order = (eight + 1.0) * math.pi
        for ref in (dens0, dens1, ddens0, ddens1, summary, centre_acc, energy_acc):
            ref[...] = jnp.zeros_like(ref)

        def harmonics(k):
            return row(b, 0, k), [row(b, 1 + m, k) for m in range(3)]

        @pl.loop(0, NEIGH, unroll=UNROLL)
        def _(k):
            w, ys = harmonics(k)
            x = row(b, 4, k)
            scale = row(b, 5, k) / x
            basis = jnp.sin(order * x) * scale
            hot = (jnp.broadcast_to(row(b, 8, k), (8, WIDE)) == eight).astype(F32)
            inputs = jnp.concatenate([basis, kind_hot[...], hot, jnp.zeros_like(hot)], axis=0)
            half = mm(w_in[...], inputs.astype(BF16))
            value, slope = silu_parts(half)
            latent = value.astype(BF16)
            lat0[k] = latent
            slope0[k] = slope.astype(BF16)
            result = mm(w_first[...], latent)
            amp[k] = result[:64]
            half0[k] = result[64:]
            env = result[32:64] * (w * 0.25)
            dens0[0] += env
            for m in range(3):
                dens0[m + 1] += env * ys[m]

        @pl.loop(0, NEIGH, unroll=UNROLL)
        def _(k):
            w, ys = harmonics(k)
            a = amp[k, 0:32]
            d = [dens0[m] for m in range(4)]
            inner = d[1] * ys[0] + d[2] * ys[1] + d[3] * ys[2]
            pieces = [a * d[0], a * inner] + [a * (d[m + 1] + ys[m] * d[0]) for m in range(3)]
            joined = jnp.concatenate(pieces, axis=0).astype(BF16)
            result = mm(w_mix[...], joined)
            tens[k] = result[256:]
            value, slope = silu_parts(half0[k] + result[:256])
            slope1[k] = slope.astype(BF16)
            latent = (lat0[k].astype(F32) + value).astype(BF16)
            lat1[k] = latent
            result = mm(w_second[...], latent)
            envl[k] = result[:32]
            half1[k] = result[32:]
            env = result[:32] * (w * 0.25)
            dens1[0] += env
            for m in range(3):
                dens1[m + 1] += env * ys[m]

        @pl.loop(0, NEIGH, unroll=UNROLL)
        def _(k):
            w, ys = harmonics(k)
            t = [tens[k, 32 * m:32 * m + 32] for m in range(4)]
            d = [dens1[m] for m in range(4)]
            joined = jnp.concatenate(
                [t[0] * d[0], t[1] * d[1] + t[2] * d[2] + t[3] * d[3]], axis=0).astype(BF16)
            value, slope = silu_parts(half1[k] + mm(w_third[...], joined))
            latent = (lat1[k].astype(F32) + value).astype(BF16).astype(F32)
            summary[...] += latent * w
            weigh = w_energy[...]
            edge = jnp.sum(latent * weigh, axis=0, keepdims=True)
            back[k, 0:1] = edge
            energy_acc[...] += jnp.broadcast_to(edge * w, (8, WIDE))
            dl2 = weigh * w
            result = mm(b_second[...], (dl2 * slope).astype(BF16))
            dlat[k] = dl2 + result[:256]
            dscal[k] = result[256:]
            ddens1[0] += result[256:288] * t[0]
            for m in range(3):
                ddens1[m + 1] += result[288:320] * t[m + 1]

        for p in range(WIDE // LANES):
            lanes = slice(p * LANES, (p + 1) * LANES)
            for half in range(2):
                flipped[lanes, half * LANES:(half + 1) * LANES] = (
                    summary[half * LANES:(half + 1) * LANES, lanes] * 0.25).T
            flipped[lanes, 2 * LANES:] = jnp.concatenate([dens1[m, :, lanes] for m in range(4)], axis=0).T

        def pack(box, rows, base):
            for r in range(4):
                for i in range(8):
                    for t in range(3):
                        box[pl.ds(base + rows * 8 * i + 3 * r + t, 8, stride=rows), :] = (
                            flipped[64 * r + 8 * i:64 * r + 8 * i + 8, t * LANES:(t + 1) * LANES])

        def post(box, target, rows, send_sem, recv_sem):
            @pl.loop(1, doms)
            def _(step):
                other = lax.rem(dom + step, doms)
                send(box.at[pl.ds(pl.multiple_of(other * rows, 8), rows)],
                     target.at[pl.ds(pl.multiple_of(dom * rows, 8), rows)], send_sem, recv_sem, (slab, other))

        @pl.when(b < 2)
        def _():
            pack(early_out, EARLY, b * 12)

        @pl.when(b == 1)
        def _():
            post(early_out, early_in, EARLY, early_send, early_recv)

        @pl.when(b == 2)
        def _():
            pack(late_out, LATE, 0)
            post(late_out, late_in, LATE, late_send, late_recv)

        @pl.loop(0, NEIGH, unroll=UNROLL)
        def _(k):
            w, ys = harmonics(k)
            q = [ddens1[m] * 0.25 for m in range(4)]
            env = envl[k]
            total = q[0] + q[1] * ys[0] + q[2] * ys[1] + q[3] * ys[2]
            dw = jnp.sum(env * total, axis=0, keepdims=True)
            env = env * w
            dy = [env * q[m + 1] for m in range(3)]
            da, db = dscal[k, 0:32], dscal[k, 32:64]
            pieces = [total * w, da * dens1[0]] + [db * dens1[m + 1] for m in range(3)]
            mixed = mm(b_mix[...], jnp.concatenate(pieces, axis=0).astype(BF16))
            dl1 = dlat[k] + mixed[:256]
            result = mm(b_first[...], (dl1 * slope1[k].astype(F32)).astype(BF16))
            dlat[k] = dl1 + result[:256]
            da = result[256:288] + mixed[256:288]
            db = result[288:320] + mixed[288:320]
            dv = [mixed[320 + 32 * m:352 + 32 * m] for m in range(3)]
            a = amp[k, 0:32]
            d = [dens0[m] for m in range(4)]
            inner = d[1] * ys[0] + d[2] * ys[1] + d[3] * ys[2]
            damp[k] = da * d[0] + db * inner + sum(dv[m] * (d[m + 1] + ys[m] * d[0]) for m in range(3))
            ba = db * a
            va = [dv[m] * a for m in range(3)]
            ddens0[0] += da * a + va[0] * ys[0] + va[1] * ys[1] + va[2] * ys[2]
            for m in range(3):
                ddens0[m + 1] += ba * ys[m] + va[m]
                dy[m] += ba * d[m + 1] + va[m] * d[0]
            back[k, 0:1] += dw
            for m in range(3):
                back[k, m + 1:m + 2] = jnp.sum(dy[m], axis=0, keepdims=True)

        @pl.loop(0, NEIGH, unroll=UNROLL)
        def _(k):
            w, ys = harmonics(k)
            q = [ddens0[m] * 0.25 for m in range(4)]
            env = amp[k, 32:64]
            total = q[0] + q[1] * ys[0] + q[2] * ys[1] + q[3] * ys[2]
            dw = back[k, 0:1] + jnp.sum(env * total, axis=0, keepdims=True)
            env = env * w
            dy = [back[k, m + 1:m + 2] + jnp.sum(env * q[m + 1], axis=0, keepdims=True) for m in range(3)]
            joined = jnp.concatenate([damp[k], total * w], axis=0).astype(BF16)
            dl0 = dlat[k] + mm(b_amp[...], joined)
            dbasis = mm(b_in[...], (dl0 * slope0[k].astype(F32)).astype(BF16))[:8]
            x, u, du, inv = row(b, 4, k), row(b, 5, k), row(b, 6, k), row(b, 7, k)
            ix = 1.0 / x
            angle = order * x
            slope = jnp.cos(angle) * order * (u * ix) + jnp.sin(angle) * ((du - u * ix) * ix)
            dx = jnp.sum(dbasis * slope, axis=0, keepdims=True) + dw * row(b, 10, k)
            dr = dx * row(b, 9, k)
            along = (ys[0] * dy[0] + ys[1] * dy[1] + ys[2] * dy[2]) * inv
            force = [ys[m] * (dr - along) + dy[m] * inv for m in range(3)]
            centre_acc[...] += jnp.concatenate(force + [jnp.zeros((5, WIDE), F32)], axis=0)
            index = near[pl.ds(k, 1), pl.ds(start, WIDE)]
            low = jnp.bitwise_and(index, LANES - 1)
            high = jnp.right_shift(index, 7)
            picker = (lax.broadcasted_iota(jnp.int32, (LANES, WIDE), 0) == low).astype(F32).astype(BF16)
            places = lax.broadcasted_iota(jnp.int32, (16, WIDE), 0) == high
            spread = [jnp.where(places, f, 0.0) for f in force]
            spread = jnp.concatenate(spread, axis=0)
            top = spread.astype(BF16)
            rest = (spread - top.astype(F32)).astype(BF16)
            both = jnp.concatenate([top, rest], axis=0)
            ghost_acc[...] += lax.dot_general(
                both, picker, (((1,), (1,)), ((), ())), preferred_element_type=F32)

        lanes = pl.ds(start, WIDE)
        grad[:, lanes] = -centre_acc[...]
        energies[:, lanes] = energy_acc[...]

    grad[:, slots:] = jnp.zeros_like(grad[:, slots:])
    for comp in range(3):
        for h in range(sub):
            lanes = slice(h * LANES, (h + 1) * LANES)
            grad[comp:comp + 1, lanes] += (
                ghost_acc[16 * comp + h:16 * comp + h + 1] + ghost_acc[48 + 16 * comp + h:49 + 16 * comp + h])
    copies = [
        send(grad.at[:, pl.ds(slots, ghosts)], back_in.at[0], back_send.at[0], back_recv.at[0], before),
        send(grad.at[:, pl.ds(slots + ghosts, ghosts)], back_in.at[1], back_send.at[1], back_recv.at[1], after),
    ]

    def settle(box, rows, sem):
        most = box.at[pl.ds(0, 63 * rows)]
        pltpu.make_async_copy(most, most, sem).wait()

    early_in[pl.ds(pl.multiple_of(dom * EARLY, 8), EARLY)] = early_out[pl.ds(pl.multiple_of(dom * EARLY, 8), EARLY)]
    late_in[pl.ds(pl.multiple_of(dom * LATE, 8), LATE)] = late_out[pl.ds(pl.multiple_of(dom * LATE, 8), LATE)]

    def select(box, rows, ranks, hots):
        found = []
        for t in range(3):
            value = jnp.concatenate([box[pl.ds(3 * r + t, 64, stride=rows), :] for r in range(ranks)], axis=0)
            found.append(sum(tn(piece, hots) for piece in parts_of(value, 2)))
        return found

    settle(early_in, EARLY, early_recv)
    for t, value in enumerate(select(early_in, EARLY, 8, home_hots[0:512])):
        feature_out[t * LANES:(t + 1) * LANES] = value

    for copy in copies:
        copy.wait()
    total = grad[:, 0:slots]
    for i in range(2):
        total = total + sum(nt(piece, picks[1 - i]) for piece in parts_of(back_in[i], 2))
    square[...] = jnp.zeros_like(square)
    rows = [-total[comp:comp + 1] for comp in range(3)] + [energies[0:1]]
    for comp in range(4):
        for p in range(slots // LANES):
            piece = rows[comp][:, p * LANES:(p + 1) * LANES]
            square[16 * comp + 2 * p:16 * comp + 2 * p + 1] = piece
            square[16 * comp + 2 * p + 1:16 * comp + 2 * p + 2] = pltpu.roll(piece, 64, 1)
    flat = square[...].T
    for d in range(64):
        force_box[d] = flat[d:d + 1]
    force_in[dom] = force_box[dom]

    @pl.loop(1, doms)
    def _(step):
        other = lax.rem(dom + step, doms)
        send(force_box.at[other], force_in.at[dom], force_send, force_recv, (slab, other))

    settle(late_in, LATE, late_recv)
    for t, value in enumerate(select(late_in, LATE, 4, home_hots[512:768])):
        feature_out[t * LANES:(t + 1) * LANES] += value
    settle(early_out, EARLY, early_send)
    settle(late_out, LATE, late_send)

    settle(force_in, 1, force_recv)
    for d in range(64):
        square[d:d + 1] = force_in[d]
    picked = sum(tn(piece, home_hot[...]) for piece in parts_of(square[0:64], 2))
    right = home_rank[...]
    result = [jnp.sum(picked[16 * comp:16 * comp + 16] * right, axis=0, keepdims=True) for comp in range(4)]
    for comp in range(3):
        force_out[comp:comp + 1] = result[comp]
    energy_out[...] = result[3].reshape(atoms)
    settle(force_box, 1, force_send)


def local(
    positions, species, domain, neighbours, ghost_lists,
    embed_weight, tensor_weight, env_weight, scalar_mix, vector_mix, latent_weight, energy_weight,
):
    slots, ghosts, atoms = neighbours.shape[1], ghost_lists.shape[1], positions.shape[1]
    blocks = slots // WIDE
    v = lambda shape, dtype=F32: pltpu.VMEM(shape, dtype)
    dma = pltpu.SemaphoreType.DMA
    scratch = [
        v((64, 1, LANES)), v((64, 1, LANES)), v((LANES, LANES)), v((2, 8, ghosts)), v((2, 8, ghosts)),
        dma, dma, dma((2,)), dma((2,)),
        v((8, 2 * slots)), v((NEIGH, slots), jnp.int32), v((2, slots, ghosts), BF16),
        v((64, atoms), BF16), v((slots, atoms), BF16), v((16, atoms)), v((WIDE, 384)),
        v((8, 2 * slots)), v((8, slots)), v((2, 8, ghosts)),
        v((64 * EARLY, LANES)), v((64 * EARLY, LANES)), v((64 * LATE, LANES)), v((64 * LATE, LANES)),
        v((64, 1, LANES)), v((64, 1, LANES)),
        dma, dma, dma, dma, dma, dma, dma((2,)), dma((2,)),
        v((256, 32), BF16), v((320, 256), BF16), v((384, 160), BF16), v((288, 256), BF16), v((256, 64), BF16),
        v((256, WIDE)), v((320, 256), BF16), v((416, 160), BF16), v((320, 256), BF16), v((256, 64), BF16),
        v((16, 256), BF16), v((128, 256)),
        v((blocks, 11, NEIGH, WIDE)), v((8, WIDE)),
        v((NEIGH, 256, WIDE), BF16), v((NEIGH, 256, WIDE), BF16), v((NEIGH, 256, WIDE)),
        v((NEIGH, 64, WIDE)), v((NEIGH, 128, WIDE)), v((NEIGH, 32, WIDE)),
        v((NEIGH, 256, WIDE), BF16), v((NEIGH, 256, WIDE), BF16), v((NEIGH, 256, WIDE)),
        v((NEIGH, 256, WIDE)), v((NEIGH, 64, WIDE)), v((NEIGH, 32, WIDE)), v((NEIGH, 8, WIDE)),
        v((4, 32, WIDE)), v((4, 32, WIDE)), v((4, 32, WIDE)), v((4, 32, WIDE)),
        v((256, WIDE)), v((96, LANES)), v((8, WIDE)), v((8, WIDE)),
    ]
    forces, atom_energy, atom_features = pl.pallas_call(
        whole_kernel,
        out_shape=(
            jax.ShapeDtypeStruct((3, atoms), F32),
            jax.ShapeDtypeStruct((atoms,), F32),
            jax.ShapeDtypeStruct((384, atoms), F32),
        ),
        in_specs=[pl.BlockSpec(memory_space=pltpu.VMEM)] * 12,
        out_specs=[pl.BlockSpec(memory_space=pltpu.VMEM)] * 3,
        scratch_shapes=scratch,
        compiler_params=pltpu.CompilerParams(
            collective_id=0, has_side_effects=True, vmem_limit_bytes=56 * 1024 * 1024),
    )(positions, species, domain.T, neighbours, ghost_lists, embed_weight, tensor_weight.T,
      env_weight.transpose(0, 2, 1), scalar_mix.T, vector_mix, latent_weight, energy_weight)
    return forces, atom_energy, atom_features


def solution(mesh):
    both = ("slab", "dom")
    in_specs = (P(None, both), P(both), P(both, None), P(None, both), P(None, both)) + (P(),) * 7
    out_specs = (P(None, both), P(both), P(None, both))
    return jax.shard_map(local, mesh=mesh, in_specs=in_specs, out_specs=out_specs, check_vma=False)
```

time: 142 us -> 103 us (0.73); the launches traced: 139 us -> 103 us
  Pallas kernels: 123 us -> 98.7 us
  local copies, waits for them, and re-layouts: 14.7 us -> 3.79 us
    pallas_call x3 -> x1, Pallas kernels: 123 us -> 98.7 us  [local(): pl.pallas_call(whole_kernel, out_shape=(jax.ShapeDtypeStruct((3, atoms),...]
    unnamed x22 -> x5, local copies, waits for them, and re-layouts: 12.8 us -> 3.79 us
    broadcast_in_dim x2 -> x0, local copies, waits for them, and re-layouts: 1.9 us -> none  [the longest x1 1.22 us: evaluate(): energy_weight[None]]
where the time goes in v2:
time: 103 us
  Pallas kernels  98.7 us (96%)
  local copies, waits for them, and re-layouts  3.79 us (4%)
    pallas_call x1, Pallas kernels, local(): pl.pallas_call(whole_kernel, out_shape=(jax.ShapeDtypeStruct((3, atoms),...  98.7 us
    unnamed x5, local copies, waits for them, and re-layouts  3.79 us

profile of v2, /device:TPU:1, one launch (start us, length us, event | category | flops | bytes accessed | tf_op | source)
XLA Modules:
  0.0 103.1 jit_solution(221187328401260734)
XLA Ops:
  0.6 98.7 %shard_map.139 = (f32[3,384]{1,0:T(4,128)}, f32[384]{0:T(512)}, f32[384,384]{1,0:T(8,128)}) custom-call(f32[3,384]{1,0:T(4,128)} %positions.1, s32[384]{0:T(512)} %species.1, s32[1,384]{1,0:T(1,128)} %bitcast.7, s32[16,768]{1,0:T(8,128)} %neighbours.1, s32[2,384]{1,0:T(2,128)} %ghost_lists.1, bf16[24,256]{1,0:T(8,128)(2,1)} %embed_weight.1, ...), custom_call_target="tpu_custom_call" | custom-call | tf_op jit(solution)/shard_map/pallas_call | solution.py:541
  99.3 0.0 copy-start
  99.3 1.3 %copy.18 = f32[3,384]{1,0:T(4,128)} copy(f32[3,384]{1,0:T(4,128)} %get-tuple-element.6) | data formatting | bytes 9216
  100.6 0.0 copy-done
  100.6 0.6 copy.19
  101.2 1.9 %copy.20 = f32[384,384]{1,0:T(8,128)} copy(f32[384,384]{1,0:T(8,128)} %get-tuple-element.8) | data formatting | bytes 1179648
Async XLA Ops:
  99.3 1.3 %copy-start = (f32[384]{0:T(512)S(1)}, f32[384]{0:T(512)}, u32[]{:S(2)}) copy-start(f32[384]{0:T(512)} %get-tuple-element.7) | copy-start | bytes 4612

commit v3 on v2

--- a/solution.py
+++ b/solution.py
@@ -10,9 +10,14 @@
 F32 = jnp.float32
 BF16 = jnp.bfloat16
 LANES = 128
+SINE = [(-1) ** i * math.pi ** (2 * i + 1) / math.factorial(2 * i + 1) for i in range(6)]
+COSINE = [(-1) ** i * math.pi ** (2 * i) / math.factorial(2 * i) for i in range(7)]
 WIDE = 256
 NEIGH = 16
-UNROLL = 4
+UNROLL = 2
+TOGETHER = 4
+SPAN = TOGETHER * WIDE
+ROUNDS = NEIGH // TOGETHER
 MESH = pl.DeviceIdType.MESH
 EXACT_PARTS = 3
 RANKS = 12
@@ -24,7 +29,22 @@
     return jnp.dot(a, b, preferred_element_type=F32)
 
 
+def sine_parts(turns):
+    whole = jnp.floor(turns + 0.5)
+    part = turns - whole
+    sign = 1.0 - 2.0 * (whole - 2.0 * jnp.floor(whole * 0.5))
+    square = part * part
+    sine = jnp.full_like(part, SINE[-1])
+    for coefficient in SINE[-2::-1]:
+        sine = sine * square + coefficient
+    cosine = jnp.full_like(part, COSINE[-1])
+    for coefficient in COSINE[-2::-1]:
+        cosine = cosine * square + coefficient
+    return sine * part * sign, cosine * sign
+
+
 def silu_parts(half):
+    half = half.astype(BF16)
     gate = jnp.tanh(half)
     rise = 1.0 + gate
     value = half * rise
@@ -256,29 +276,38 @@
         for c, item in enumerate(items):
             geo[b, c, :, lanes] = item
 
+    def side_by_side(pieces):
+        return jnp.concatenate(pieces, axis=1)
+
     def row(b, c, k):
-        return geo[b, c, pl.ds(k, 1), :]
+        return side_by_side([geo[b, c, pl.ds(k * TOGETHER + i, 1), :] for i in range(TOGETHER)])
+
+    def tiled(value):
+        return side_by_side([value] * TOGETHER)
+
+    def folded(value):
+        return sum(value[:, i * WIDE:(i + 1) * WIDE] for i in range(TOGETHER))
 
     @pl.loop(0, blocks)
     def _(b):
         start = pl.multiple_of(b * WIDE, WIDE)
-        eight = lax.broadcasted_iota(jnp.int32, (8, WIDE), 0).astype(F32)
-        my_kind = own[3:4, pl.ds(start, WIDE)]
-        kind_hot[...] = (jnp.broadcast_to(my_kind, (8, WIDE)) == eight).astype(F32)
-        order = (eight + 1.0) * math.pi
+        eight = lax.broadcasted_iota(jnp.int32, (8, SPAN), 0).astype(F32)
+        my_kind = tiled(own[3:4, pl.ds(start, WIDE)])
+        kind_hot[...] = (jnp.broadcast_to(my_kind, (8, SPAN)) == eight).astype(F32)
+        order = eight + 1.0
         for ref in (dens0, dens1, ddens0, ddens1, summary, centre_acc, energy_acc):
             ref[...] = jnp.zeros_like(ref)
 
         def harmonics(k):
             return row(b, 0, k), [row(b, 1 + m, k) for m in range(3)]
 
-        @pl.loop(0, NEIGH, unroll=UNROLL)
+        @pl.loop(0, ROUNDS, unroll=UNROLL)
         def _(k):
             w, ys = harmonics(k)
             x = row(b, 4, k)
             scale = row(b, 5, k) / x
-            basis = jnp.sin(order * x) * scale
-            hot = (jnp.broadcast_to(row(b, 8, k), (8, WIDE)) == eight).astype(F32)
+            basis = sine_parts(order * x)[0] * scale
+            hot = (jnp.broadcast_to(row(b, 8, k), (8, SPAN)) == eight).astype(F32)
             inputs = jnp.concatenate([basis, kind_hot[...], hot, jnp.zeros_like(hot)], axis=0)
             half = mm(w_in[...], inputs.astype(BF16))
             value, slope = silu_parts(half)
@@ -287,55 +316,55 @@
             slope0[k] = slope.astype(BF16)
             result = mm(w_first[...], latent)
             amp[k] = result[:64]
-            half0[k] = result[64:]
+            half0[k] = result[64:].astype(BF16)
             env = result[32:64] * (w * 0.25)
-            dens0[0] += env
+            dens0[0] += folded(env)
             for m in range(3):
-                dens0[m + 1] += env * ys[m]
-
-        @pl.loop(0, NEIGH, unroll=UNROLL)
+                dens0[m + 1] += folded(env * ys[m])
+
+        @pl.loop(0, ROUNDS, unroll=UNROLL)
         def _(k):
             w, ys = harmonics(k)
             a = amp[k, 0:32]
-            d = [dens0[m] for m in range(4)]
+            d = [tiled(dens0[m]) for m in range(4)]
             inner = d[1] * ys[0] + d[2] * ys[1] + d[3] * ys[2]
             pieces = [a * d[0], a * inner] + [a * (d[m + 1] + ys[m] * d[0]) for m in range(3)]
             joined = jnp.concatenate(pieces, axis=0).astype(BF16)
             result = mm(w_mix[...], joined)
             tens[k] = result[256:]
-            value, slope = silu_parts(half0[k] + result[:256])
+            value, slope = silu_parts(half0[k] + result[:256].astype(BF16))
             slope1[k] = slope.astype(BF16)
-            latent = (lat0[k].astype(F32) + value).astype(BF16)
+            latent = lat0[k] + value
             lat1[k] = latent
             result = mm(w_second[...], latent)
             envl[k] = result[:32]
-            half1[k] = result[32:]
+            half1[k] = result[32:].astype(BF16)
             env = result[:32] * (w * 0.25)
-            dens1[0] += env
+            dens1[0] += folded(env)
             for m in range(3):
-                dens1[m + 1] += env * ys[m]
-
-        @pl.loop(0, NEIGH, unroll=UNROLL)
+                dens1[m + 1] += folded(env * ys[m])
+
+        @pl.loop(0, ROUNDS, unroll=UNROLL)
         def _(k):
             w, ys = harmonics(k)
             t = [tens[k, 32 * m:32 * m + 32] for m in range(4)]
-            d = [dens1[m] for m in range(4)]
+            d = [tiled(dens1[m]) for m in range(4)]
             joined = jnp.concatenate(
                 [t[0] * d[0], t[1] * d[1] + t[2] * d[2] + t[3] * d[3]], axis=0).astype(BF16)
-            value, slope = silu_parts(half1[k] + mm(w_third[...], joined))
-            latent = (lat1[k].astype(F32) + value).astype(BF16).astype(F32)
-            summary[...] += latent * w
-            weigh = w_energy[...]
+            value, slope = silu_parts(half1[k] + mm(w_third[...], joined).astype(BF16))
+            latent = (lat1[k] + value).astype(BF16).astype(F32)
+            summary[...] += folded(latent * w)
+            weigh = tiled(w_energy[...])
             edge = jnp.sum(latent * weigh, axis=0, keepdims=True)
             back[k, 0:1] = edge
-            energy_acc[...] += jnp.broadcast_to(edge * w, (8, WIDE))
-            dl2 = weigh * w
+            energy_acc[...] += jnp.broadcast_to(folded(edge * w), (8, WIDE))
+            dl2 = (weigh * w).astype(BF16)
             result = mm(b_second[...], (dl2 * slope).astype(BF16))
-            dlat[k] = dl2 + result[:256]
+            dlat[k] = dl2 + result[:256].astype(BF16)
             dscal[k] = result[256:]
-            ddens1[0] += result[256:288] * t[0]
+            ddens1[0] += folded(result[256:288] * t[0])
             for m in range(3):
-                ddens1[m + 1] += result[288:320] * t[m + 1]
+                ddens1[m + 1] += folded(result[288:320] * t[m + 1])
 
         for p in range(WIDE // LANES):
             lanes = slice(p * LANES, (p + 1) * LANES)
@@ -371,64 +400,65 @@
             pack(late_out, LATE, 0)
             post(late_out, late_in, LATE, late_send, late_recv)
 
-        @pl.loop(0, NEIGH, unroll=UNROLL)
+        @pl.loop(0, ROUNDS, unroll=UNROLL)
         def _(k):
             w, ys = harmonics(k)
-            q = [ddens1[m] * 0.25 for m in range(4)]
+            q = [tiled(ddens1[m] * 0.25) for m in range(4)]
             env = envl[k]
             total = q[0] + q[1] * ys[0] + q[2] * ys[1] + q[3] * ys[2]
             dw = jnp.sum(env * total, axis=0, keepdims=True)
             env = env * w
             dy = [env * q[m + 1] for m in range(3)]
             da, db = dscal[k, 0:32], dscal[k, 32:64]
-            pieces = [total * w, da * dens1[0]] + [db * dens1[m + 1] for m in range(3)]
+            pieces = [total * w, da * tiled(dens1[0])] + [db * tiled(dens1[m + 1]) for m in range(3)]
             mixed = mm(b_mix[...], jnp.concatenate(pieces, axis=0).astype(BF16))
-            dl1 = dlat[k] + mixed[:256]
-            result = mm(b_first[...], (dl1 * slope1[k].astype(F32)).astype(BF16))
-            dlat[k] = dl1 + result[:256]
+            dl1 = dlat[k] + mixed[:256].astype(BF16)
+            result = mm(b_first[...], (dl1 * slope1[k]))
+            dlat[k] = dl1 + result[:256].astype(BF16)
             da = result[256:288] + mixed[256:288]
             db = result[288:320] + mixed[288:320]
             dv = [mixed[320 + 32 * m:352 + 32 * m] for m in range(3)]
             a = amp[k, 0:32]
-            d = [dens0[m] for m in range(4)]
+            d = [tiled(dens0[m]) for m in range(4)]
             inner = d[1] * ys[0] + d[2] * ys[1] + d[3] * ys[2]
             damp[k] = da * d[0] + db * inner + sum(dv[m] * (d[m + 1] + ys[m] * d[0]) for m in range(3))
             ba = db * a
             va = [dv[m] * a for m in range(3)]
-            ddens0[0] += da * a + va[0] * ys[0] + va[1] * ys[1] + va[2] * ys[2]
+            ddens0[0] += folded(da * a + va[0] * ys[0] + va[1] * ys[1] + va[2] * ys[2])
             for m in range(3):
-                ddens0[m + 1] += ba * ys[m] + va[m]
+                ddens0[m + 1] += folded(ba * ys[m] + va[m])
                 dy[m] += ba * d[m + 1] + va[m] * d[0]
             back[k, 0:1] += dw
             for m in range(3):
                 back[k, m + 1:m + 2] = jnp.sum(dy[m], axis=0, keepdims=True)
 
-        @pl.loop(0, NEIGH, unroll=UNROLL)
+        @pl.loop(0, ROUNDS, unroll=UNROLL)
         def _(k):
             w, ys = harmonics(k)
-            q = [ddens0[m] * 0.25 for m in range(4)]
+            q = [tiled(ddens0[m] * 0.25) for m in range(4)]
             env = amp[k, 32:64]
             total = q[0] + q[1] * ys[0] + q[2] * ys[1] + q[3] * ys[2]
             dw = back[k, 0:1] + jnp.sum(env * total, axis=0, keepdims=True)
             env = env * w
             dy = [back[k, m + 1:m + 2] + jnp.sum(env * q[m + 1], axis=0, keepdims=True) for m in range(3)]
             joined = jnp.concatenate([damp[k], total * w], axis=0).astype(BF16)
-            dl0 = dlat[k] + mm(b_amp[...], joined)
-            dbasis = mm(b_in[...], (dl0 * slope0[k].astype(F32)).astype(BF16))[:8]
+            dl0 = dlat[k] + mm(b_amp[...], joined).astype(BF16)
+            dbasis = mm(b_in[...], (dl0 * slope0[k]))[:8]
             x, u, du, inv = row(b, 4, k), row(b, 5, k), row(b, 6, k), row(b, 7, k)
             ix = 1.0 / x
-            angle = order * x
-            slope = jnp.cos(angle) * order * (u * ix) + jnp.sin(angle) * ((du - u * ix) * ix)
+            sine, cosine = sine_parts(order * x)
+            slope = cosine * order * (math.pi * u * ix) + sine * ((du - u * ix) * ix)
             dx = jnp.sum(dbasis * slope, axis=0, keepdims=True) + dw * row(b, 10, k)
             dr = dx * row(b, 9, k)
             along = (ys[0] * dy[0] + ys[1] * dy[1] + ys[2] * dy[2]) * inv
             force = [ys[m] * (dr - along) + dy[m] * inv for m in range(3)]
-            centre_acc[...] += jnp.concatenate(force + [jnp.zeros((5, WIDE), F32)], axis=0)
-            index = near[pl.ds(k, 1), pl.ds(start, WIDE)]
+            centre_acc[...] += folded(jnp.concatenate(force + [jnp.zeros((5, SPAN), F32)], axis=0))
+            index = side_by_side(
+                [near[pl.ds(k * TOGETHER + i, 1), pl.ds(start, WIDE)] for i in range(TOGETHER)])
             low = jnp.bitwise_and(index, LANES - 1)
             high = jnp.right_shift(index, 7)
-            picker = (lax.broadcasted_iota(jnp.int32, (LANES, WIDE), 0) == low).astype(F32).astype(BF16)
-            places = lax.broadcasted_iota(jnp.int32, (16, WIDE), 0) == high
+            picker = (lax.broadcasted_iota(jnp.int32, (LANES, SPAN), 0) == low).astype(F32).astype(BF16)
+            places = lax.broadcasted_iota(jnp.int32, (16, SPAN), 0) == high
             spread = [jnp.where(places, f, 0.0) for f in force]
             spread = jnp.concatenate(spread, axis=0)
             top = spread.astype(BF16)
@@ -530,11 +560,11 @@
         v((256, 32), BF16), v((320, 256), BF16), v((384, 160), BF16), v((288, 256), BF16), v((256, 64), BF16),
         v((256, WIDE)), v((320, 256), BF16), v((416, 160), BF16), v((320, 256), BF16), v((256, 64), BF16),
         v((16, 256), BF16), v((128, 256)),
-        v((blocks, 11, NEIGH, WIDE)), v((8, WIDE)),
-        v((NEIGH, 256, WIDE), BF16), v((NEIGH, 256, WIDE), BF16), v((NEIGH, 256, WIDE)),
-        v((NEIGH, 64, WIDE)), v((NEIGH, 128, WIDE)), v((NEIGH, 32, WIDE)),
-        v((NEIGH, 256, WIDE), BF16), v((NEIGH, 256, WIDE), BF16), v((NEIGH, 256, WIDE)),
-        v((NEIGH, 256, WIDE)), v((NEIGH, 64, WIDE)), v((NEIGH, 32, WIDE)), v((NEIGH, 8, WIDE)),
+        v((blocks, 11, NEIGH, WIDE)), v((8, SPAN)),
+        v((ROUNDS, 256, SPAN), BF16), v((ROUNDS, 256, SPAN), BF16), v((ROUNDS, 256, SPAN), BF16),
+        v((ROUNDS, 64, SPAN)), v((ROUNDS, 128, SPAN)), v((ROUNDS, 32, SPAN)),
+        v((ROUNDS, 256, SPAN), BF16), v((ROUNDS, 256, SPAN), BF16), v((ROUNDS, 256, SPAN), BF16),
+        v((ROUNDS, 256, SPAN), BF16), v((ROUNDS, 64, SPAN)), v((ROUNDS, 32, SPAN)), v((ROUNDS, 8, SPAN)),
         v((4, 32, WIDE)), v((4, 32, WIDE)), v((4, 32, WIDE)), v((4, 32, WIDE)),
         v((256, WIDE)), v((96, LANES)), v((8, WIDE)), v((8, WIDE)),
     ]

time: 103 us -> 86.2 us (0.84)
  Pallas kernels: 98.7 us -> 81.6 us
    pallas_call x1, Pallas kernels: 98.7 us -> 81.6 us  [local(): pl.pallas_call(whole_kernel, out_shape=(jax.ShapeDtypeStruct((3, atoms),...]
where the time goes in v3:
time: 86.2 us; the launch traced here: 86 us
  Pallas kernels  81.6 us (95%)
  local copies, waits for them, and re-layouts  3.79 us (4%)
    pallas_call x1, Pallas kernels, local(): pl.pallas_call(whole_kernel, out_shape=(jax.ShapeDtypeStruct((3, atoms),...  81.6 us
    unnamed x5, local copies, waits for them, and re-layouts  3.79 us

profile of v3, /device:TPU:1, one launch (start us, length us, event | category | flops | bytes accessed | tf_op | source)
XLA Modules:
  0.0 86.0 jit_solution(14410745137834240218)
XLA Ops:
  0.6 81.6 %shard_map.139 = (f32[3,384]{1,0:T(4,128)}, f32[384]{0:T(512)}, f32[384,384]{1,0:T(8,128)}) custom-call(f32[3,384]{1,0:T(4,128)} %positions.1, s32[384]{0:T(512)} %species.1, s32[1,384]{1,0:T(1,128)} %bitcast.7, s32[16,768]{1,0:T(8,128)} %neighbours.1, s32[2,384]{1,0:T(2,128)} %ghost_lists.1, bf16[24,256]{1,0:T(8,128)(2,1)} %embed_weight.1, ...), custom_call_target="tpu_custom_call" | custom-call | tf_op jit(solution)/shard_map/pallas_call | solution.py:571
  82.2 0.0 copy-start
  82.2 1.3 %copy.18 = f32[3,384]{1,0:T(4,128)} copy(f32[3,384]{1,0:T(4,128)} %get-tuple-element.6) | data formatting | bytes 9216
  83.5 0.0 copy-done
  83.5 0.6 copy.19
  84.1 1.9 %copy.20 = f32[384,384]{1,0:T(8,128)} copy(f32[384,384]{1,0:T(8,128)} %get-tuple-element.8) | data formatting | bytes 1179648
Async XLA Ops:
  82.2 1.3 %copy-start = (f32[384]{0:T(512)S(1)}, f32[384]{0:T(512)}, u32[]{:S(2)}) copy-start(f32[384]{0:T(512)} %get-tuple-element.7) | copy-start | bytes 4612

commit v4 on v3

--- a/solution.py
+++ b/solution.py
@@ -21,8 +21,8 @@
 MESH = pl.DeviceIdType.MESH
 EXACT_PARTS = 3
 RANKS = 12
-EARLY = 24
-LATE = 16
+PARTS = (8, 16, 16)
+SENDS = 7
 
 
 def mm(a, b):
@@ -82,7 +82,7 @@
 def greet(slab, dom, doms, before, after):
     barrier = pltpu.get_barrier_semaphore()
 
-    @pl.loop(1, doms)
+    @pl.loop(1, doms, unroll=SENDS)
     def _(step):
         pl.semaphore_signal(
             barrier, inc=1, device_id=(slab, lax.rem(dom + step, doms)), device_id_type=MESH)
@@ -143,18 +143,24 @@
     w_mix[width:] = core[:, 0:160].astype(BF16)
 
 
+def locate(row):
+    part = 0 if row < 8 else 1 if row < 24 else 2
+    return part, row - (0, 8, 24)[part]
+
+
 def whole_kernel(
     positions, species, domain, neighbours, ghost_lists,
     embed_weight, tensor_turned, env_turned, scalar_turned, vector_mix, latent_weight, energy_weight,
     force_out, energy_out, feature_out,
     outbox, inbox, square, lend, arrive, box_send, box_recv, ghost_send, ghost_recv,
     ext, near, picks, home_hot, home_hots, home_rank, flipped, grad, energies, back_in,
-    early_out, early_in, late_out, late_in, force_box, force_in,
-    early_send, early_recv, late_send, late_recv, force_send, force_recv, back_send, back_recv,
+    out_a, out_b, out_c, in_a, in_b, in_c, force_box, force_in,
+    part_send, part_recv, force_send, force_recv, back_send, back_recv,
     w_in, w_first, w_mix, w_second, w_third, w_energy, b_second, b_mix, b_first, b_amp, b_in, stage,
     geo, kind_hot, lat0, slope0, half0, amp, tens, envl, lat1, slope1, half1, dlat, dscal, damp, back,
     dens0, dens1, ddens0, ddens1, summary, ghost_acc, centre_acc, energy_acc,
 ):
+    part_out, part_in = (out_a, out_b, out_c), (in_a, in_b, in_c)
     slab, dom, doms, before, after = partners()
     barrier = greet(slab, dom, doms, before, after)
     atoms = positions.shape[1]
@@ -183,7 +189,7 @@
 
     pl.semaphore_wait(barrier, doms + 1)
 
-    @pl.loop(1, doms)
+    @pl.loop(1, doms, unroll=SENDS)
     def _(step):
         other = lax.rem(dom + step, doms)
         send(outbox.at[other], inbox.at[dom], box_send, box_recv, (slab, other))
@@ -191,14 +197,6 @@
     code = jnp.where(lane == 0, target.astype(F32), jnp.where(lane == 1, rank, 0.0))
     code = code.T
     target, rank = code[0:1], code[1:2]
-    hot = (lax.broadcasted_iota(jnp.int32, (64, atoms), 0).astype(F32) == target).astype(F32)
-    home_hot[...] = hot.astype(BF16)
-    for r in range(RANKS):
-        home_hots[64 * r:64 * r + 64] = jnp.where(rank == float(r), hot, 0.0).astype(BF16)
-    home_rank[...] = (lax.broadcasted_iota(jnp.int32, (16, atoms), 0).astype(F32) == rank).astype(F32)
-    arrange_weights(
-        embed_weight, tensor_turned, env_turned, scalar_turned, vector_mix, latent_weight, energy_weight,
-        w_in, w_first, w_mix, w_second, w_third, w_energy, b_second, b_mix, b_first, b_amp, b_in, stage)
     index = neighbours[...]
     pieces = jnp.concatenate(
         [jnp.right_shift(index, 7).astype(F32), jnp.bitwise_and(index, LANES - 1).astype(F32)], axis=0)
@@ -228,11 +226,20 @@
             odd = rolled[16 * c + 2 * p + 1:16 * c + 2 * p + 2]
             both = jnp.where(first, even, odd)
             ext[c:c + 1, p * LANES:(p + 1) * LANES] = both - 1.0 if c == 3 else both
-    own = parts_of(ext[:, 0:slots], EXACT_PARTS)
+    own = jnp.concatenate(parts_of(ext[:, 0:slots], EXACT_PARTS), axis=0)
     copies = []
     for i, other in ((0, before), (1, after)):
-        lend[i] = sum(mm(piece, picks[i]) for piece in own)
+        value = mm(own, picks[i])
+        lend[i] = value[0:8] + value[8:16] + value[16:24]
         copies.append(send(lend.at[i], arrive.at[i], ghost_send.at[i], ghost_recv.at[i], other))
+    hot = (lax.broadcasted_iota(jnp.int32, (64, atoms), 0).astype(F32) == target).astype(F32)
+    home_hot[...] = hot.astype(BF16)
+    for r in range(RANKS):
+        home_hots[64 * r:64 * r + 64] = jnp.where(rank == float(r), hot, 0.0).astype(BF16)
+    home_rank[...] = (lax.broadcasted_iota(jnp.int32, (16, atoms), 0).astype(F32) == rank).astype(F32)
+    arrange_weights(
+        embed_weight, tensor_turned, env_turned, scalar_turned, vector_mix, latent_weight, energy_weight,
+        w_in, w_first, w_mix, w_second, w_third, w_energy, b_second, b_mix, b_first, b_amp, b_in, stage)
     pltpu.make_async_copy(outbox.at[pl.ds(0, 63)], outbox.at[pl.ds(0, 63)], box_send).wait()
     for copy in copies:
         copy.wait()
@@ -295,8 +302,12 @@
         my_kind = tiled(own[3:4, pl.ds(start, WIDE)])
         kind_hot[...] = (jnp.broadcast_to(my_kind, (8, SPAN)) == eight).astype(F32)
         order = eight + 1.0
-        for ref in (dens0, dens1, ddens0, ddens1, summary, centre_acc, energy_acc):
+        at, base = b * ROUNDS, 4 * b
+        for ref in (dens0, dens1, ddens1):
+            ref[pl.ds(base, 4)] = jnp.zeros((4,) + ref.shape[1:], F32)
+        for ref in (summary, energy_acc):
             ref[...] = jnp.zeros_like(ref)
+
 
         def harmonics(k):
             return row(b, 0, k), [row(b, 1 + m, k) for m in range(3)]
@@ -313,42 +324,42 @@
             value, slope = silu_parts(half)
             latent = value.astype(BF16)
             lat0[k] = latent
-            slope0[k] = slope.astype(BF16)
+            slope0[at + k] = slope.astype(BF16)
             result = mm(w_first[...], latent)
-            amp[k] = result[:64]
+            amp[at + k] = result[:64]
             half0[k] = result[64:].astype(BF16)
             env = result[32:64] * (w * 0.25)
-            dens0[0] += folded(env)
+            dens0[base + 0] += folded(env)
             for m in range(3):
-                dens0[m + 1] += folded(env * ys[m])
+                dens0[base + m + 1] += folded(env * ys[m])
 
         @pl.loop(0, ROUNDS, unroll=UNROLL)
         def _(k):
             w, ys = harmonics(k)
-            a = amp[k, 0:32]
-            d = [tiled(dens0[m]) for m in range(4)]
+            a = amp[at + k, 0:32]
+            d = [tiled(dens0[base + m]) for m in range(4)]
             inner = d[1] * ys[0] + d[2] * ys[1] + d[3] * ys[2]
             pieces = [a * d[0], a * inner] + [a * (d[m + 1] + ys[m] * d[0]) for m in range(3)]
             joined = jnp.concatenate(pieces, axis=0).astype(BF16)
             result = mm(w_mix[...], joined)
             tens[k] = result[256:]
             value, slope = silu_parts(half0[k] + result[:256].astype(BF16))
-            slope1[k] = slope.astype(BF16)
+            slope1[at + k] = slope.astype(BF16)
             latent = lat0[k] + value
             lat1[k] = latent
             result = mm(w_second[...], latent)
-            envl[k] = result[:32]
+            envl[at + k] = result[:32]
             half1[k] = result[32:].astype(BF16)
             env = result[:32] * (w * 0.25)
-            dens1[0] += folded(env)
+            dens1[base + 0] += folded(env)
             for m in range(3):
-                dens1[m + 1] += folded(env * ys[m])
+                dens1[base + m + 1] += folded(env * ys[m])
 
         @pl.loop(0, ROUNDS, unroll=UNROLL)
         def _(k):
             w, ys = harmonics(k)
             t = [tens[k, 32 * m:32 * m + 32] for m in range(4)]
-            d = [tiled(dens1[m]) for m in range(4)]
+            d = [tiled(dens1[base + m]) for m in range(4)]
             joined = jnp.concatenate(
                 [t[0] * d[0], t[1] * d[1] + t[2] * d[2] + t[3] * d[3]], axis=0).astype(BF16)
             value, slope = silu_parts(half1[k] + mm(w_third[...], joined).astype(BF16))
@@ -356,70 +367,83 @@
             summary[...] += folded(latent * w)
             weigh = tiled(w_energy[...])
             edge = jnp.sum(latent * weigh, axis=0, keepdims=True)
-            back[k, 0:1] = edge
+            back[at + k, 0:1] = edge
             energy_acc[...] += jnp.broadcast_to(folded(edge * w), (8, WIDE))
             dl2 = (weigh * w).astype(BF16)
             result = mm(b_second[...], (dl2 * slope).astype(BF16))
-            dlat[k] = dl2 + result[:256].astype(BF16)
-            dscal[k] = result[256:]
-            ddens1[0] += folded(result[256:288] * t[0])
+            dlat[at + k] = dl2 + result[:256].astype(BF16)
+            dscal[at + k] = result[256:]
+            ddens1[base + 0] += folded(result[256:288] * t[0])
             for m in range(3):
-                ddens1[m + 1] += folded(result[288:320] * t[m + 1])
+                ddens1[base + m + 1] += folded(result[288:320] * t[m + 1])
 
         for p in range(WIDE // LANES):
             lanes = slice(p * LANES, (p + 1) * LANES)
             for half in range(2):
                 flipped[lanes, half * LANES:(half + 1) * LANES] = (
                     summary[half * LANES:(half + 1) * LANES, lanes] * 0.25).T
-            flipped[lanes, 2 * LANES:] = jnp.concatenate([dens1[m, :, lanes] for m in range(4)], axis=0).T
-
-        def pack(box, rows, base):
+            flipped[lanes, 2 * LANES:] = jnp.concatenate([dens1[base + m, :, lanes] for m in range(4)], axis=0).T
+
+        def pack(place):
             for r in range(4):
-                for i in range(8):
-                    for t in range(3):
-                        box[pl.ds(base + rows * 8 * i + 3 * r + t, 8, stride=rows), :] = (
+                for t in range(3):
+                    part, row = place(3 * r + t)
+                    rows = PARTS[part]
+                    for i in range(8):
+                        part_out[part][pl.ds(rows * 8 * i + row, 8, stride=rows), :] = (
                             flipped[64 * r + 8 * i:64 * r + 8 * i + 8, t * LANES:(t + 1) * LANES])
 
-        def post(box, target, rows, send_sem, recv_sem):
-            @pl.loop(1, doms)
+        def post(part):
+            rows = PARTS[part]
+
+            @pl.loop(1, doms, unroll=SENDS)
             def _(step):
                 other = lax.rem(dom + step, doms)
-                send(box.at[pl.ds(pl.multiple_of(other * rows, 8), rows)],
-                     target.at[pl.ds(pl.multiple_of(dom * rows, 8), rows)], send_sem, recv_sem, (slab, other))
-
-        @pl.when(b < 2)
-        def _():
-            pack(early_out, EARLY, b * 12)
-
-        @pl.when(b == 1)
-        def _():
-            post(early_out, early_in, EARLY, early_send, early_recv)
-
-        @pl.when(b == 2)
-        def _():
-            pack(late_out, LATE, 0)
-            post(late_out, late_in, LATE, late_send, late_recv)
+                send(part_out[part].at[pl.ds(pl.multiple_of(other * rows, 8), rows)],
+                     part_in[part].at[pl.ds(pl.multiple_of(dom * rows, 8), rows)],
+                     part_send.at[part], part_recv.at[part], (slab, other))
+
+        for block in range(3):
+            @pl.when(b == block)
+            def _(block=block):
+                pack(lambda row: locate(12 * block + row))
+                post(block)
+
+        energies[:, pl.ds(start, WIDE)] = energy_acc[...]
+
+    @pl.loop(0, blocks)
+    def _(b):
+        start = pl.multiple_of(b * WIDE, WIDE)
+        eight = lax.broadcasted_iota(jnp.int32, (8, SPAN), 0).astype(F32)
+        order = eight + 1.0
+        at, base = b * ROUNDS, 4 * b
+        for ref in (ddens0, centre_acc):
+            ref[...] = jnp.zeros_like(ref)
+
+
+        def harmonics(k):
+            return row(b, 0, k), [row(b, 1 + m, k) for m in range(3)]
 
         @pl.loop(0, ROUNDS, unroll=UNROLL)
         def _(k):
             w, ys = harmonics(k)
-            q = [tiled(ddens1[m] * 0.25) for m in range(4)]
-            env = envl[k]
+            q = [tiled(ddens1[base + m] * 0.25) for m in range(4)]
+            env = envl[at + k]
             total = q[0] + q[1] * ys[0] + q[2] * ys[1] + q[3] * ys[2]
             dw = jnp.sum(env * total, axis=0, keepdims=True)
             env = env * w
             dy = [env * q[m + 1] for m in range(3)]
-            da, db = dscal[k, 0:32], dscal[k, 32:64]
-            pieces = [total * w, da * tiled(dens1[0])] + [db * tiled(dens1[m + 1]) for m in range(3)]
+            da, db = dscal[at + k, 0:32], dscal[at + k, 32:64]
+            pieces = [total * w, da * tiled(dens1[base + 0])] + [db * tiled(dens1[base + m + 1]) for m in range(3)]
             mixed = mm(b_mix[...], jnp.concatenate(pieces, axis=0).astype(BF16))
-            dl1 = dlat[k] + mixed[:256].astype(BF16)
-            result = mm(b_first[...], (dl1 * slope1[k]))
-            dlat[k] = dl1 + result[:256].astype(BF16)
+            dl1 = dlat[at + k] + mixed[:256].astype(BF16)
+            result = mm(b_first[...], (dl1 * slope1[at + k]))
+            dlat[at + k] = dl1 + result[:256].astype(BF16)
             da = result[256:288] + mixed[256:288]
             db = result[288:320] + mixed[288:320]
             dv = [mixed[320 + 32 * m:352 + 32 * m] for m in range(3)]
-            a = amp[k, 0:32]
-            d = [tiled(dens0[m]) for m in range(4)]
+            a = amp[at + k, 0:32]
+            d = [tiled(dens0[base + m]) for m in range(4)]
             inner = d[1] * ys[0] + d[2] * ys[1] + d[3] * ys[2]
             damp[k] = da * d[0] + db * inner + sum(dv[m] * (d[m + 1] + ys[m] * d[0]) for m in range(3))
             ba = db * a
@@ -428,22 +452,22 @@
             for m in range(3):
                 ddens0[m + 1] += folded(ba * ys[m] + va[m])
                 dy[m] += ba * d[m + 1] + va[m] * d[0]
-            back[k, 0:1] += dw
+            back[at + k, 0:1] += dw
             for m in range(3):
-                back[k, m + 1:m + 2] = jnp.sum(dy[m], axis=0, keepdims=True)
+                back[at + k, m + 1:m + 2] = jnp.sum(dy[m], axis=0, keepdims=True)
 
         @pl.loop(0, ROUNDS, unroll=UNROLL)
         def _(k):
             w, ys = harmonics(k)
             q = [tiled(ddens0[m] * 0.25) for m in range(4)]
-            env = amp[k, 32:64]
+            env = amp[at + k, 32:64]
             total = q[0] + q[1] * ys[0] + q[2] * ys[1] + q[3] * ys[2]
-            dw = back[k, 0:1] + jnp.sum(env * total, axis=0, keepdims=True)
+            dw = back[at + k, 0:1] + jnp.sum(env * total, axis=0, keepdims=True)
             env = env * w
-            dy = [back[k, m + 1:m + 2] + jnp.sum(env * q[m + 1], axis=0, keepdims=True) for m in range(3)]
+            dy = [back[at + k, m + 1:m + 2] + jnp.sum(env * q[m + 1], axis=0, keepdims=True) for m in range(3)]
             joined = jnp.concatenate([damp[k], total * w], axis=0).astype(BF16)
-            dl0 = dlat[k] + mm(b_amp[...], joined).astype(BF16)
-            dbasis = mm(b_in[...], (dl0 * slope0[k]))[:8]
+            dl0 = dlat[at + k] + mm(b_amp[...], joined).astype(BF16)
+            dbasis = mm(b_in[...], (dl0 * slope0[at + k]))[:8]
             x, u, du, inv = row(b, 4, k), row(b, 5, k), row(b, 6, k), row(b, 7, k)
             ix = 1.0 / x
             sine, cosine = sine_parts(order * x)
@@ -467,9 +491,7 @@
             ghost_acc[...] += lax.dot_general(
                 both, picker, (((1,), (1,)), ((), ())), preferred_element_type=F32)
 
-        lanes = pl.ds(start, WIDE)
-        grad[:, lanes] = -centre_acc[...]
-        energies[:, lanes] = energy_acc[...]
+        grad[:, pl.ds(start, WIDE)] = -centre_acc[...]
 
     grad[:, slots:] = jnp.zeros_like(grad[:, slots:])
     for comp in range(3):
@@ -486,25 +508,34 @@
         most = box.at[pl.ds(0, 63 * rows)]
         pltpu.make_async_copy(most, most, sem).wait()
 
-    early_in[pl.ds(pl.multiple_of(dom * EARLY, 8), EARLY)] = early_out[pl.ds(pl.multiple_of(dom * EARLY, 8), EARLY)]
-    late_in[pl.ds(pl.multiple_of(dom * LATE, 8), LATE)] = late_out[pl.ds(pl.multiple_of(dom * LATE, 8), LATE)]
-
-    def select(box, rows, ranks, hots):
+    for part, rows in enumerate(PARTS):
+        mine = pl.ds(pl.multiple_of(dom * rows, 8), rows)
+        part_in[part][mine] = part_out[part][mine]
+
+    def select(ranks):
         found = []
         for t in range(3):
-            value = jnp.concatenate([box[pl.ds(3 * r + t, 64, stride=rows), :] for r in range(ranks)], axis=0)
-            found.append(sum(tn(piece, hots) for piece in parts_of(value, 2)))
-        return found
-
-    settle(early_in, EARLY, early_recv)
-    for t, value in enumerate(select(early_in, EARLY, 8, home_hots[0:512])):
+            pieces = []
+            for r in ranks:
+                part, row = locate(3 * r + t)
+                pieces.append(part_in[part][pl.ds(row, 64, stride=PARTS[part]), :])
+            found += parts_of(jnp.concatenate(pieces, axis=0), 2)
+        hots = home_hots[64 * ranks[0]:64 * ranks[-1] + 64]
+        value = tn(jnp.concatenate(found, axis=1), hots)
+        return [value[2 * t * LANES:(2 * t + 1) * LANES] + value[(2 * t + 1) * LANES:(2 * t + 2) * LANES]
+                for t in range(3)]
+
+    settle(in_a, PARTS[0], part_recv.at[0])
+    settle(in_b, PARTS[1], part_recv.at[1])
+    for t, value in enumerate(select(range(8))):
         feature_out[t * LANES:(t + 1) * LANES] = value
 
     for copy in copies:
         copy.wait()
     total = grad[:, 0:slots]
     for i in range(2):
-        total = total + sum(nt(piece, picks[1 - i]) for piece in parts_of(back_in[i], 2))
+        value = nt(jnp.concatenate(parts_of(back_in[i], 2), axis=0), picks[1 - i])
+        total = total + value[:8] + value[8:]
     square[...] = jnp.zeros_like(square)
     rows = [-total[comp:comp + 1] for comp in range(3)] + [energies[0:1]]
     for comp in range(4):
@@ -517,16 +548,16 @@
         force_box[d] = flat[d:d + 1]
     force_in[dom] = force_box[dom]
 
-    @pl.loop(1, doms)
+    @pl.loop(1, doms, unroll=SENDS)
     def _(step):
         other = lax.rem(dom + step, doms)
         send(force_box.at[other], force_in.at[dom], force_send, force_recv, (slab, other))
 
-    settle(late_in, LATE, late_recv)
-    for t, value in enumerate(select(late_in, LATE, 4, home_hots[512:768])):
+    settle(in_c, PARTS[2], part_recv.at[2])
+    for t, value in enumerate(select(range(8, RANKS))):
         feature_out[t * LANES:(t + 1) * LANES] += value
-    settle(early_out, EARLY, early_send)
-    settle(late_out, LATE, late_send)
+    for part, rows in enumerate(PARTS):
+        settle(part_out[part], rows, part_send.at[part])
 
     settle(force_in, 1, force_recv)
     for d in range(64):
@@ -554,18 +585,19 @@
         v((8, 2 * slots)), v((NEIGH, slots), jnp.int32), v((2, slots, ghosts), BF16),
         v((64, atoms), BF16), v((slots, atoms), BF16), v((16, atoms)), v((WIDE, 384)),
         v((8, 2 * slots)), v((8, slots)), v((2, 8, ghosts)),
-        v((64 * EARLY, LANES)), v((64 * EARLY, LANES)), v((64 * LATE, LANES)), v((64 * LATE, LANES)),
+        *[v((64 * rows, LANES)) for rows in PARTS], *[v((64 * rows, LANES)) for rows in PARTS],
         v((64, 1, LANES)), v((64, 1, LANES)),
-        dma, dma, dma, dma, dma, dma, dma((2,)), dma((2,)),
+        dma((3,)), dma((3,)), dma, dma, dma((2,)), dma((2,)),
         v((256, 32), BF16), v((320, 256), BF16), v((384, 160), BF16), v((288, 256), BF16), v((256, 64), BF16),
         v((256, WIDE)), v((320, 256), BF16), v((416, 160), BF16), v((320, 256), BF16), v((256, 64), BF16),
         v((16, 256), BF16), v((128, 256)),
         v((blocks, 11, NEIGH, WIDE)), v((8, SPAN)),
-        v((ROUNDS, 256, SPAN), BF16), v((ROUNDS, 256, SPAN), BF16), v((ROUNDS, 256, SPAN), BF16),
-        v((ROUNDS, 64, SPAN)), v((ROUNDS, 128, SPAN)), v((ROUNDS, 32, SPAN)),
-        v((ROUNDS, 256, SPAN), BF16), v((ROUNDS, 256, SPAN), BF16), v((ROUNDS, 256, SPAN), BF16),
-        v((ROUNDS, 256, SPAN), BF16), v((ROUNDS, 64, SPAN)), v((ROUNDS, 32, SPAN)), v((ROUNDS, 8, SPAN)),
-        v((4, 32, WIDE)), v((4, 32, WIDE)), v((4, 32, WIDE)), v((4, 32, WIDE)),
+        v((ROUNDS, 256, SPAN), BF16), v((blocks * ROUNDS, 256, SPAN), BF16), v((ROUNDS, 256, SPAN), BF16),
+        v((blocks * ROUNDS, 64, SPAN)), v((ROUNDS, 128, SPAN)), v((blocks * ROUNDS, 32, SPAN)),
+        v((ROUNDS, 256, SPAN), BF16), v((blocks * ROUNDS, 256, SPAN), BF16), v((ROUNDS, 256, SPAN), BF16),
+        v((blocks * ROUNDS, 256, SPAN), BF16), v((blocks * ROUNDS, 64, SPAN)), v((ROUNDS, 32, SPAN)),
+        v((blocks * ROUNDS, 8, SPAN)),
+        v((4 * blocks, 32, WIDE)), v((4 * blocks, 32, WIDE)), v((4, 32, WIDE)), v((4 * blocks, 32, WIDE)),
         v((256, WIDE)), v((96, LANES)), v((8, WIDE)), v((8, WIDE)),
     ]
     forces, atom_energy, atom_features = pl.pallas_call(

time: 86.2 us -> 78.2 us (0.907)
  Pallas kernels: 81.6 us -> 73.2 us
    pallas_call x1, Pallas kernels: 81.6 us -> 73.2 us  [local(): pl.pallas_call(whole_kernel, out_shape=(jax.ShapeDtypeStruct((3, atoms),...]
where the time goes in v4:
time: 78.2 us; the launch traced here: 77.6 us
  Pallas kernels  73.2 us (94%)
  local copies, waits for them, and re-layouts  3.79 us (5%)
    pallas_call x1, Pallas kernels, local(): pl.pallas_call(whole_kernel, out_shape=(jax.ShapeDtypeStruct((3, atoms),...  73.2 us
    unnamed x5, local copies, waits for them, and re-layouts  3.79 us

profile of v4, /device:TPU:1, one launch (start us, length us, event | category | flops | bytes accessed | tf_op | source)
XLA Modules:
  0.0 77.6 jit_solution(3458628668518415792)
XLA Ops:
  0.6 73.2 %shard_map.139 = (f32[3,384]{1,0:T(4,128)}, f32[384]{0:T(512)}, f32[384,384]{1,0:T(8,128)}) custom-call(f32[3,384]{1,0:T(4,128)} %positions.1, s32[384]{0:T(512)} %species.1, s32[1,384]{1,0:T(1,128)} %bitcast.7, s32[16,768]{1,0:T(8,128)} %neighbours.1, s32[2,384]{1,0:T(2,128)} %ghost_lists.1, bf16[24,256]{1,0:T(8,128)(2,1)} %embed_weight.1, ...), custom_call_target="tpu_custom_call" | custom-call | tf_op jit(solution)/shard_map/pallas_call | solution.py:603
  73.8 0.0 copy-start
  73.9 1.3 %copy.18 = f32[3,384]{1,0:T(4,128)} copy(f32[3,384]{1,0:T(4,128)} %get-tuple-element.6) | data formatting | bytes 9216
  75.1 0.0 copy-done
  75.1 0.6 copy.19
  75.7 1.9 %copy.20 = f32[384,384]{1,0:T(8,128)} copy(f32[384,384]{1,0:T(8,128)} %get-tuple-element.8) | data formatting | bytes 1179648
Async XLA Ops:
  73.8 1.3 %copy-start = (f32[384]{0:T(512)S(1)}, f32[384]{0:T(512)}, u32[]{:S(2)}) copy-start(f32[384]{0:T(512)} %get-tuple-element.7) | copy-start | bytes 4612

commit v5 on v4

--- a/solution.py
+++ b/solution.py
@@ -14,8 +14,8 @@
 COSINE = [(-1) ** i * math.pi ** (2 * i) / math.factorial(2 * i) for i in range(7)]
 WIDE = 256
 NEIGH = 16
-UNROLL = 2
-TOGETHER = 4
+UNROLL = 1
+TOGETHER = 8
 SPAN = TOGETHER * WIDE
 ROUNDS = NEIGH // TOGETHER
 MESH = pl.DeviceIdType.MESH

time: 78.2 us -> 76.1 us (0.973)
  Pallas kernels: 73.2 us -> 71.2 us
    pallas_call x1, Pallas kernels: 73.2 us -> 71.2 us  [local(): pl.pallas_call(whole_kernel, out_shape=(jax.ShapeDtypeStruct((3, atoms),...]
where the time goes in v5:
time: 76.1 us; the launch traced here: 75.7 us
  Pallas kernels  71.2 us (94%)
  local copies, waits for them, and re-layouts  3.79 us (5%)
    pallas_call x1, Pallas kernels, local(): pl.pallas_call(whole_kernel, out_shape=(jax.ShapeDtypeStruct((3, atoms),...  71.2 us
    unnamed x5, local copies, waits for them, and re-layouts  3.79 us

profile of v5, /device:TPU:1, one launch (start us, length us, event | category | flops | bytes accessed | tf_op | source)
XLA Modules:
  0.0 75.7 jit_solution(2490717127510369813)
XLA Ops:
  0.6 71.2 %shard_map.139 = (f32[3,384]{1,0:T(4,128)}, f32[384]{0:T(512)}, f32[384,384]{1,0:T(8,128)}) custom-call(f32[3,384]{1,0:T(4,128)} %positions.1, s32[384]{0:T(512)} %species.1, s32[1,384]{1,0:T(1,128)} %bitcast.7, s32[16,768]{1,0:T(8,128)} %neighbours.1, s32[2,384]{1,0:T(2,128)} %ghost_lists.1, bf16[24,256]{1,0:T(8,128)(2,1)} %embed_weight.1, ...), custom_call_target="tpu_custom_call" | custom-call | tf_op jit(solution)/shard_map/pallas_call | solution.py:603
  71.9 0.0 copy-start
  71.9 1.3 %copy.18 = f32[3,384]{1,0:T(4,128)} copy(f32[3,384]{1,0:T(4,128)} %get-tuple-element.6) | data formatting | bytes 9216
  73.2 0.0 copy-done
  73.2 0.6 copy.19
  73.8 1.9 %copy.20 = f32[384,384]{1,0:T(8,128)} copy(f32[384,384]{1,0:T(8,128)} %get-tuple-element.8) | data formatting | bytes 1179648
Async XLA Ops:
  71.9 1.3 %copy-start = (f32[384]{0:T(512)S(1)}, f32[384]{0:T(512)}, u32[]{:S(2)}) copy-start(f32[384]{0:T(512)} %get-tuple-element.7) | copy-start | bytes 4612

commit v6 on v5

--- a/solution.py
+++ b/solution.py
@@ -519,11 +519,10 @@
             for r in ranks:
                 part, row = locate(3 * r + t)
                 pieces.append(part_in[part][pl.ds(row, 64, stride=PARTS[part]), :])
-            found += parts_of(jnp.concatenate(pieces, axis=0), 2)
+            found.append(jnp.concatenate(pieces, axis=0).astype(BF16))
         hots = home_hots[64 * ranks[0]:64 * ranks[-1] + 64]
         value = tn(jnp.concatenate(found, axis=1), hots)
-        return [value[2 * t * LANES:(2 * t + 1) * LANES] + value[(2 * t + 1) * LANES:(2 * t + 2) * LANES]
-                for t in range(3)]
+        return [value[t * LANES:(t + 1) * LANES] for t in range(3)]
 
     settle(in_a, PARTS[0], part_recv.at[0])
     settle(in_b, PARTS[1], part_recv.at[1])

time: 76.1 us -> 76.1 us (level)
  no operation moved by 1% of the time
where the time goes in v6:
time: 76.1 us; the launch traced here: 75.7 us
  Pallas kernels  71.2 us (94%)
  local copies, waits for them, and re-layouts  3.79 us (5%)
    pallas_call x1, Pallas kernels, local(): pl.pallas_call(whole_kernel, out_shape=(jax.ShapeDtypeStruct((3, atoms),...  71.2 us
    unnamed x5, local copies, waits for them, and re-layouts  3.79 us

profile of v6, /device:TPU:1, one launch (start us, length us, event | category | flops | bytes accessed | tf_op | source)
XLA Modules:
  0.0 75.7 jit_solution(1307688844933761186)
XLA Ops:
  0.6 71.2 %shard_map.139 = (f32[3,384]{1,0:T(4,128)}, f32[384]{0:T(512)}, f32[384,384]{1,0:T(8,128)}) custom-call(f32[3,384]{1,0:T(4,128)} %positions.1, s32[384]{0:T(512)} %species.1, s32[1,384]{1,0:T(1,128)} %bitcast.7, s32[16,768]{1,0:T(8,128)} %neighbours.1, s32[2,384]{1,0:T(2,128)} %ghost_lists.1, bf16[24,256]{1,0:T(8,128)(2,1)} %embed_weight.1, ...), custom_call_target="tpu_custom_call" | custom-call | tf_op jit(solution)/shard_map/pallas_call | solution.py:602
  71.9 0.0 copy-start
  71.9 1.3 %copy.18 = f32[3,384]{1,0:T(4,128)} copy(f32[3,384]{1,0:T(4,128)} %get-tuple-element.6) | data formatting | bytes 9216
  73.2 0.0 copy-done
  73.2 0.6 copy.19
  73.8 1.9 %copy.20 = f32[384,384]{1,0:T(8,128)} copy(f32[384,384]{1,0:T(8,128)} %get-tuple-element.8) | data formatting | bytes 1179648
Async XLA Ops:
  71.9 1.3 %copy-start = (f32[384]{0:T(512)S(1)}, f32[384]{0:T(512)}, u32[]{:S(2)}) copy-start(f32[384]{0:T(512)} %get-tuple-element.7) | copy-start | bytes 4612
